TPU v7x, 256 devices: a whole 4x4x8 slice. The times are simulated.
256 devices in a mesh: seq: 2 (over core), fsdp: 128 (over x, z, y).
Axes of the slice: x: 4, y: 4, z: 8, core: 2. Of those that a mesh axis runs over, the one named last changes fastest.
Arguments:
- hidden: bfloat16 [128, 512, 768], P('fsdp', 'seq'), may hold values from -24 to 24
- d_out: bfloat16 [128, 512, 768], P('fsdp', 'seq'), may hold values from -24 to 24
- lengths: int32 [128, 2], P('fsdp'), may hold values from 1 to 12, 16 in all within a row
- slot_source: int32 [128, 512], P('fsdp'), may hold values from 0 to 511, each once within a row
- first_gain: bfloat16 [768], P('fsdp'), may hold values from 0.099609375 to 1.8984375
- qkv_weight: bfloat16 [768, 2304], P('fsdp'), may hold values from -0.21875 to 0.21875
- out_weight: bfloat16 [768, 768], P(None, 'fsdp'), may hold values from -2 to 2
- second_gain: bfloat16 [768], P('fsdp'), may hold values from 0.099609375 to 1.8984375
- up_weight: bfloat16 [768, 3072], P('fsdp'), may hold values from -0.21875 to 0.21875
- up_bias: bfloat16 [3072], P('fsdp'), may hold values from -3 to 3
- down_weight: bfloat16 [3072, 768], P(None, 'fsdp'), may hold values from -0.109375 to 0.109375
- down_bias: bfloat16 [768], P('fsdp'), may hold values from -3 to 3
Outputs:
- output: bfloat16 [128, 512, 768], P('fsdp', 'seq')
- grad_hidden: float32 [128, 512, 768], P('fsdp', 'seq')
- grad_first_gain: float32 [768], P('fsdp')
- grad_qkv: float32 [768, 2304], P('fsdp')
- grad_out: float32 [768, 768], P(None, 'fsdp')
- grad_second_gain: float32 [768], P('fsdp')
- grad_up: float32 [768, 3072], P('fsdp')
- grad_up_bias: float32 [3072], P('fsdp')
- grad_down: float32 [3072, 768], P(None, 'fsdp')
- grad_down_bias: float32 [768], P('fsdp')
Inputs may be any that keep to these rules, and one draw needn't show every extreme that they name: `lengths`: each row lists whole sequences in blocks of 16 tokens; it sums to 16 and no entry exceeds 12. `slot_source`: each row is a permutation of the group's rows.
All inputs are finite; a program needn't handle non-finite values.
Results may differ from a plain program's by a relative error of at most 0.017.
Values may be sent and summed in bfloat16 or wider, within the bound.
A program may use at most 192 MiB of HBM per device.

v0:
```python
from functools import partial

import jax
import jax.numpy as jnp
from jax import lax
from jax.sharding import PartitionSpec as P

HEADS = 12
HD = 64
BLOCK = 16


EPS = 1e-05
NEG = -1e30


def normalize(values):
    row_mean = jnp.mean(values, axis=-1, keepdims=True)
    centered = values - row_mean
    variance = jnp.mean(centered * centered, axis=-1, keepdims=True)
    inv_scale = lax.rsqrt(variance + EPS)
    return (centered * inv_scale, inv_scale)


def normalize_back(grad_normed, normed, inv_scale):
    mean_grad = jnp.mean(grad_normed, axis=-1, keepdims=True)
    mean_cross = jnp.mean(grad_normed * normed, axis=-1, keepdims=True)
    return inv_scale * (grad_normed - mean_grad - normed * mean_cross)


def token_tables(lengths_row, clean):
    blocks = jnp.arange(clean, dtype=jnp.int32) // BLOCK
    starts = jnp.cumsum(lengths_row) - lengths_row
    begins = jnp.max(jnp.where(starts[None, :] <= blocks[:, None], starts[None, :], 0), axis=1)
    segment = jnp.sum((starts[None, 1:] <= blocks[:, None]).astype(jnp.int32), axis=1)
    position = (jnp.arange(clean, dtype=jnp.int32) - BLOCK * begins).astype(jnp.float32)
    frequency = jnp.power(10000.0, -2.0 * jnp.arange(HD // 2, dtype=jnp.float32) / HD)
    angles = position[:, None] * frequency[None, :]
    return (jnp.cos(angles), jnp.sin(angles), segment, blocks)


def rotate(values, cosine, sine):
    half = values.shape[-1] // 2
    first = values[..., :half]
    second = values[..., half:]
    return jnp.concatenate(
        [first * cosine - second * sine, first * sine + second * cosine], axis=-1
    )


def rotate_back(grads_in, cosine, sine):
    half = grads_in.shape[-1] // 2
    first = grads_in[..., :half]
    second = grads_in[..., half:]
    return jnp.concatenate(
        [first * cosine + second * sine, second * cosine - first * sine], axis=-1
    )


def allowed(query_meta, key_meta):
    query_seg, query_blk, query_noisy = query_meta
    key_seg, key_blk, key_noisy = key_meta
    same_segment = query_seg[:, None] == key_seg[None, :]
    q_block = query_blk[:, None]
    k_block = key_blk[None, :]
    q_noisy = query_noisy[:, None]
    k_noisy = key_noisy[None, :]
    block_rule = (
        q_noisy & k_noisy & (k_block == q_block)
        | q_noisy & ~k_noisy & (k_block < q_block)
        | ~q_noisy & ~k_noisy & (k_block <= q_block)
    )
    return same_segment & block_rule


def key_slices(array, ranges, axis):
    return jnp.concatenate(
        [lax.slice_in_dim(array, start, start + size, axis=axis) for start, size in ranges],
        axis=axis,
    )


def head_forward(query_head, key_head, value_head, pairs, scale):
    scores = (
        jnp.einsum("qd,kd->qk", query_head, key_head, preferred_element_type=jnp.float32) * scale
    )
    scores = jnp.where(pairs, scores, NEG)
    row_max = jnp.max(scores, axis=-1, keepdims=True)
    exps = jnp.exp(scores - row_max)
    row_total = jnp.sum(exps, axis=-1, keepdims=True)
    probs = (exps / row_total).astype(jnp.bfloat16)
    attended = jnp.dot(probs, value_head, preferred_element_type=jnp.float32).astype(jnp.bfloat16)
    return (attended, (row_max + jnp.log(row_total))[:, 0])


def head_backward(query_head, key_head, value_head, grad_head, log_total, pairs, scale):
    scores = (
        jnp.einsum("qd,kd->qk", query_head, key_head, preferred_element_type=jnp.float32) * scale
    )
    scores = jnp.where(pairs, scores, NEG)
    probs = jnp.exp(scores - log_total[:, None])
    grad_probs = jnp.einsum("qd,kd->qk", grad_head, value_head, preferred_element_type=jnp.float32)
    row_delta = jnp.sum(probs * grad_probs, axis=-1, keepdims=True)
    grad_scores = (probs * (grad_probs - row_delta)).astype(jnp.bfloat16)
    grad_query = jnp.dot(grad_scores, key_head, preferred_element_type=jnp.float32) * scale
    grad_key = (
        jnp.einsum("qk,qd->kd", grad_scores, query_head, preferred_element_type=jnp.float32) * scale
    )
    grad_value = jnp.einsum(
        "qk,qd->kd", probs.astype(jnp.bfloat16), grad_head, preferred_element_type=jnp.float32
    )
    return (grad_query, grad_key, grad_value)


def unpack(gathered):
    return tuple(
        (member.astype(jnp.float32) if member.ndim == 1 else member for member in gathered)
    )


def owner_major(grad_full, shard_dim, owners):
    if shard_dim == 0:
        return grad_full.reshape(owners, -1)
    leading = grad_full.shape[0]
    return grad_full.reshape(leading, owners, -1).transpose(1, 0, 2).reshape(owners, -1)


def per_device(
    hidden,
    d_out,
    lengths,
    slot_source,
    first_gain,
    qkv_weight,
    out_weight,
    second_gain,
    up_weight,
    up_bias,
    down_weight,
    down_bias,
):
    gathered = (
        lax.all_gather(first_gain, "fsdp", axis=0, tiled=True),
        lax.all_gather(qkv_weight, "fsdp", axis=0, tiled=True),
        lax.all_gather(out_weight, "fsdp", axis=1, tiled=True),
        lax.all_gather(second_gain, "fsdp", axis=0, tiled=True),
        lax.all_gather(up_weight, "fsdp", axis=0, tiled=True),
        lax.all_gather(up_bias, "fsdp", axis=0, tiled=True),
        lax.all_gather(down_weight, "fsdp", axis=1, tiled=True),
        lax.all_gather(down_bias, "fsdp", axis=0, tiled=True),
    )
    gain_one, qkv_mat, out_mat, gain_two, up_mat, up_vec, down_mat, down_vec = unpack(gathered)
    seq_count = lax.axis_size("seq")
    owners = lax.axis_size("fsdp")
    row_count = hidden.shape[1]
    width = hidden.shape[2]
    pack_rows = slot_source.shape[1]
    clean = pack_rows // 2
    local_heads = HEADS // seq_count
    head_cols = local_heads * HD
    scale = HD ** (-0.5)
    seq_order = slot_source[0]
    inverse = (
        jnp.zeros((pack_rows,), jnp.int32).at[seq_order].set(jnp.arange(pack_rows, dtype=jnp.int32))
    )
    cosine, sine, segment, blocks = token_tables(lengths[0], clean)
    cos_slot = jnp.concatenate([cosine, cosine])[None]
    sin_slot = jnp.concatenate([sine, sine])[None]
    slot_meta = (
        jnp.concatenate([segment, segment]),
        jnp.concatenate([blocks, blocks]),
        jnp.arange(pack_rows) < clean,
    )
    inputs = hidden[0].astype(jnp.float32)
    normed_one, inv_one = normalize(inputs)
    ln_one = (normed_one * gain_one).astype(jnp.bfloat16)
    qkv_rows = jnp.dot(ln_one, qkv_mat, preferred_element_type=jnp.float32).astype(jnp.bfloat16)
    qkv_heads = lax.all_to_all(
        qkv_rows.reshape(row_count, 3, seq_count, head_cols),
        "seq",
        split_axis=2,
        concat_axis=0,
        tiled=True,
    )
    qkv_seq = jnp.take(qkv_heads.reshape(pack_rows, 3, head_cols), seq_order, axis=0)
    queries = qkv_seq[:, 0].reshape(pack_rows, local_heads, HD).transpose(1, 0, 2)
    keys_all = qkv_seq[:, 1].reshape(pack_rows, local_heads, HD).transpose(1, 0, 2)
    values_seq = qkv_seq[:, 2].reshape(pack_rows, local_heads, HD).transpose(1, 0, 2)
    rot_queries = rotate(queries.astype(jnp.float32), cos_slot, sin_slot).astype(jnp.bfloat16)
    rot_keys = rotate(keys_all.astype(jnp.float32), cos_slot, sin_slot).astype(jnp.bfloat16)
    span = min(512, clean)
    block_plan = [(0, ((0, span), (clean, span)))]
    block_plan += [(clean, ((clean, span),))]
    attended_list = []
    total_list = []
    pair_list = []
    for query_start, ranges in block_plan:
        query_meta = tuple((member[query_start : query_start + span] for member in slot_meta))
        key_meta = tuple((key_slices(member, ranges, 0) for member in slot_meta))
        pairs = allowed(query_meta, key_meta)
        pair_list.append(pairs)
        query_block = rot_queries[:, query_start : query_start + span]
        key_block = key_slices(rot_keys, ranges, 1)
        value_block = key_slices(values_seq, ranges, 1)
        attended, log_total = lax.map(
            lambda per_head: head_forward(per_head[0], per_head[1], per_head[2], pairs, scale),
            (query_block, key_block, value_block),
        )
        attended_list.append(attended)
        total_list.append(log_total)
    attended_seq = jnp.concatenate(attended_list, axis=1)
    log_totals = jnp.concatenate(total_list, axis=1)
    attended_given = jnp.take(
        attended_seq.transpose(1, 0, 2).reshape(pack_rows, head_cols), inverse, axis=0
    )
    attention = lax.all_to_all(
        attended_given.reshape(pack_rows, 1, head_cols),
        "seq",
        split_axis=0,
        concat_axis=1,
        tiled=True,
    ).reshape(row_count, width)
    middle = inputs + jnp.dot(attention, out_mat, preferred_element_type=jnp.float32)
    normed_two, inv_two = normalize(middle)
    ln_two = (normed_two * gain_two).astype(jnp.bfloat16)
    pre_act = jnp.dot(ln_two, up_mat, preferred_element_type=jnp.float32) + up_vec
    act, gelu_back = jax.vjp(partial(jax.nn.gelu, approximate=True), pre_act)
    act_low = act.astype(jnp.bfloat16)
    result = middle + jnp.dot(act_low, down_mat, preferred_element_type=jnp.float32) + down_vec
    output = result.astype(jnp.bfloat16)
    gathered = (
        lax.all_gather(first_gain, "fsdp", axis=0, tiled=True),
        lax.all_gather(qkv_weight, "fsdp", axis=0, tiled=True),
        lax.all_gather(out_weight, "fsdp", axis=1, tiled=True),
        lax.all_gather(second_gain, "fsdp", axis=0, tiled=True),
        lax.all_gather(up_weight, "fsdp", axis=0, tiled=True),
        lax.all_gather(up_bias, "fsdp", axis=0, tiled=True),
        lax.all_gather(down_weight, "fsdp", axis=1, tiled=True),
        lax.all_gather(down_bias, "fsdp", axis=0, tiled=True),
    )
    gain_one, qkv_mat, out_mat, gain_two, up_mat, up_vec, down_mat, down_vec = unpack(gathered)
    grad_output = d_out[0]
    grad_output_f = grad_output.astype(jnp.float32)
    grad_down_bias = jnp.sum(grad_output_f, axis=0)
    grad_down = jnp.einsum("rf,rd->fd", act_low, grad_output, preferred_element_type=jnp.float32)
    grad_act = jnp.einsum("rd,fd->rf", grad_output, down_mat, preferred_element_type=jnp.float32)
    grad_pre = gelu_back(grad_act)[0].astype(jnp.bfloat16)
    grad_up_bias = jnp.sum(grad_pre.astype(jnp.float32), axis=0)
    grad_up = jnp.einsum("rd,rf->df", ln_two, grad_pre, preferred_element_type=jnp.float32)
    grad_ln_two = jnp.einsum("rf,df->rd", grad_pre, up_mat, preferred_element_type=jnp.float32)
    grad_second_gain = jnp.sum(grad_ln_two * normed_two, axis=0)
    grad_middle = grad_output_f + normalize_back(grad_ln_two * gain_two, normed_two, inv_two)
    grad_mid_low = grad_middle.astype(jnp.bfloat16)
    grad_out = jnp.einsum("rc,rd->cd", attention, grad_mid_low, preferred_element_type=jnp.float32)
    grad_attention = jnp.einsum(
        "rd,cd->rc", grad_mid_low, out_mat, preferred_element_type=jnp.float32
    ).astype(jnp.bfloat16)
    grad_heads = lax.all_to_all(
        grad_attention.reshape(row_count, seq_count, head_cols),
        "seq",
        split_axis=1,
        concat_axis=0,
        tiled=True,
    )
    grad_seq = (
        jnp.take(grad_heads.reshape(pack_rows, head_cols), seq_order, axis=0)
        .reshape(pack_rows, local_heads, HD)
        .transpose(1, 0, 2)
    )
    query_grads = []
    grad_keys = jnp.zeros((local_heads, pack_rows, HD), jnp.float32)
    grad_values = jnp.zeros((local_heads, pack_rows, HD), jnp.float32)
    for plan_index in range(len(block_plan)):
        query_start, ranges = block_plan[plan_index]
        pairs = pair_list[plan_index]
        query_block = rot_queries[:, query_start : query_start + span]
        grad_block = grad_seq[:, query_start : query_start + span]
        total_block = log_totals[:, query_start : query_start + span]
        key_block = key_slices(rot_keys, ranges, 1)
        value_block = key_slices(values_seq, ranges, 1)
        grad_query, grad_key, grad_value = lax.map(
            lambda per_head: head_backward(
                per_head[0], per_head[1], per_head[2], per_head[3], per_head[4], pairs, scale
            ),
            (query_block, key_block, value_block, grad_block, total_block),
        )
        query_grads.append(grad_query)
        offset = 0
        for start, size in ranges:
            grad_keys = grad_keys.at[:, start : start + size].add(
                grad_key[:, offset : offset + size]
            )
            grad_values = grad_values.at[:, start : start + size].add(
                grad_value[:, offset : offset + size]
            )
            offset = offset + size
    grad_queries = rotate_back(jnp.concatenate(query_grads, axis=1), cos_slot, sin_slot)
    grad_keys = rotate_back(grad_keys, cos_slot, sin_slot)
    grad_stack = (
        jnp.stack([grad_queries, grad_keys, grad_values], axis=0)
        .transpose(2, 0, 1, 3)
        .reshape(pack_rows, 3, head_cols)
        .astype(jnp.bfloat16)
    )
    grad_given = jnp.take(grad_stack, inverse, axis=0).reshape(pack_rows, 3, 1, head_cols)
    grad_rows = lax.all_to_all(grad_given, "seq", split_axis=0, concat_axis=2, tiled=True).reshape(
        row_count, 3 * width
    )
    grad_qkv = jnp.einsum("rd,re->de", ln_one, grad_rows, preferred_element_type=jnp.float32)
    grad_ln_one = jnp.einsum("re,de->rd", grad_rows, qkv_mat, preferred_element_type=jnp.float32)
    grad_first_gain = jnp.sum(grad_ln_one * normed_one, axis=0)
    grad_input = grad_middle + normalize_back(grad_ln_one * gain_one, normed_one, inv_one)
    matrix_list = [
        owner_major(grad_qkv, 0, owners),
        owner_major(grad_out, 1, owners),
        owner_major(grad_up, 0, owners),
        owner_major(grad_down, 1, owners),
    ]
    matrix_pack = jnp.concatenate(matrix_list, axis=1)
    matrix_cols = matrix_pack.shape[1]
    matrix_pack = matrix_pack.reshape(owners * 8, matrix_cols // 8)
    vector_pack = jnp.concatenate(
        [
            owner_major(grad_first_gain, 0, owners),
            owner_major(grad_second_gain, 0, owners),
            owner_major(grad_up_bias, 0, owners),
            owner_major(grad_down_bias, 0, owners),
        ],
        axis=1,
    )
    owned = (
        lax.psum_scatter(matrix_pack, "fsdp", scatter_dimension=0, tiled=True),
        lax.psum_scatter(vector_pack, "fsdp", scatter_dimension=0, tiled=True),
    )
    summed = (
        lax.psum(owned[0].astype(jnp.bfloat16), "seq").astype(jnp.float32),
        lax.psum(owned[1].astype(jnp.bfloat16), "seq").astype(jnp.float32),
    )
    matrix_flat = summed[0].reshape(-1)
    vector_flat = summed[1].reshape(-1)
    width_part = width // owners
    ff_part = grad_up.shape[1] // owners
    ff_total = grad_up.shape[1]
    sizes_list = [
        width_part * 3 * width,
        width * width_part,
        width_part * ff_total,
        ff_total * width_part,
    ]
    offsets_list = [
        0,
        sizes_list[0],
        sizes_list[0] + sizes_list[1],
        sizes_list[0] + sizes_list[1] + sizes_list[2],
    ]
    own_qkv = matrix_flat[offsets_list[0] : offsets_list[0] + sizes_list[0]].reshape(
        width_part, 3 * width
    )
    own_out = matrix_flat[offsets_list[1] : offsets_list[1] + sizes_list[1]].reshape(
        width, width_part
    )
    own_up = matrix_flat[offsets_list[2] : offsets_list[2] + sizes_list[2]].reshape(
        width_part, ff_total
    )
    own_down = matrix_flat[offsets_list[3] : offsets_list[3] + sizes_list[3]].reshape(
        ff_total, width_part
    )
    own_gain_one = vector_flat[0:width_part]
    own_gain_two = vector_flat[width_part : 2 * width_part]
    own_up_bias = vector_flat[2 * width_part : 2 * width_part + ff_part]
    own_down_bias = vector_flat[2 * width_part + ff_part : 3 * width_part + ff_part]
    return (
        output[None],
        grad_input[None],
        own_gain_one,
        own_qkv,
        own_out,
        own_gain_two,
        own_up,
        own_up_bias,
        own_down,
        own_down_bias,
    )


def solution(mesh):
    return jax.shard_map(
        per_device,
        mesh=mesh,
        in_specs=(
            P("fsdp", "seq", None),
            P("fsdp", "seq", None),
            P("fsdp", None),
            P("fsdp", None),
            P("fsdp"),
            P("fsdp", None),
            P(None, "fsdp"),
            P("fsdp"),
            P("fsdp", None),
            P("fsdp"),
            P(None, "fsdp"),
            P("fsdp"),
        ),
        out_specs=(
            P("fsdp", "seq", None),
            P("fsdp", "seq", None),
            P("fsdp"),
            P("fsdp", None),
            P(None, "fsdp"),
            P("fsdp"),
            P("fsdp", None),
            P("fsdp"),
            P(None, "fsdp"),
            P("fsdp"),
        ),
        check_vma=False,
    )
```

profile of v0, /device:TPU:1, one launch (start us, length us, event | category | flops | bytes accessed | tf_op | source)
XLA Modules:
  0.0 2027.8 jit_solution(30461698873556691)
XLA Ops:
  14.9 2.4 scatter_custom_fusion
  29.3 584.4 %all-reduce.5 = (bf16[3072]{0:T(1024)(128)(2,1)S(1)}, bf16[768]{0:T(1024)(128)(2,1)S(1)}, bf16[768]{0:T(1024)(128)(2,1)S(1)}, bf16[768]{0:T(1024)(128)(2,1)}) all-reduce(bf16[3072]{0:T(1024)(128)(2,1)S(1)} %dynamic-update-slice.22, bf16[768]{0:T(1024)(128)(2,1)S(1)} %dynamic-update-slice.20, ...), channel_id=1, replica_groups=mesh['seq'=2,'fsdp'=128] {'fsdp'}, use_global_device_ids=true, to_apply=%add.2 | all-reduce | flops 5376 | bytes 21504
  617.3 2.3 reshape.608
  619.7 6.7 reshape.606
  626.4 4.2 convolution_convert_fusion.2
  630.5 2.7 reshape.524
  633.4 114.9 %all_to_all.60 = bf16[256,3,2,384]{3,0,1,2:T(8,128)(2,1)S(1)} all-to-all(bf16[256,3,2,384]{3,0,1,2:T(8,128)(2,1)S(1)} %copy.241), channel_id=1, replica_groups=mesh['seq'=2,'fsdp'=128] {'seq'}, dimensions={2} | all-to-all | bytes 2359296 | tf_op jit(solution)/shard_map/all_to_all | solution.py:178
  748.4 2.2 copy.243
  750.6 4.8 gather_fusion
  755.4 1.7 copy_select_fusion
  763.3 1.9 add_convert_fusion.2
  766.4 1.8 fusion.137
  769.7 1.9 copy.251
  772.3 12.8 while.67
  785.9 16.4 while.66
  804.3 1.9 gather_fusion.1
  807.9 4.3 all_to_all.61
  813.7 7.8 reshape.610
  821.5 5.4 convolution_add_fusion
  826.9 7.8 reshape.612
  834.7 7.2 convert_reduce_fusion
  842.0 4.5 multiply_reduce_fusion.2
  846.5 5.1 fusion.147
  851.7 2.4 convert_bitcast_fusion.1
  855.5 4.4 all_to_all.62
  859.9 1.9 gather_fusion.2
  862.5 31.7 %while.69 = (s32[]{:T(128)}, f32[6,256,64]{1,2,0:T(8,128)S(1)}, f32[6,256,64]{1,2,0:T(8,128)S(1)}, f32[6,256,64]{1,2,0:T(8,128)S(1)}, bf16[6,256,64]{2,1,0:T(8,1...) while((s32[]{:T(128)}, f32[6,256,64]{1,2,0:T(8,128)S(1)}, ...), condition=%wide.region_22.25_spmd.clone.clone, body=%wide.region_20.24_spmd.clone.sunk.clone | while | flops 43417344 | bytes 2572425 | solution.py:281
  895.2 43.4 %while.68 = (s32[]{:T(128)}, f32[6,256,64]{1,2,0:T(8,128)S(1)}, f32[6,512,64]{1,2,0:T(8,128)}, f32[6,512,64]{1,2,0:T(8,128)}, bf16[6,256,64]{2,1,0:T(8,128)(2,1)...) while((s32[]{:T(128)}, f32[6,256,64]{1,2,0:T(8,128)S(1)}, ...), condition=%wide.region_19.22_spmd.clone.clone, body=%wide.region_17.21_spmd.clone.sunk.clone | while | flops 86818560 | bytes 4867753 | solution.py:281
  897.0 1.6 multiply_reduce_fusion.11
  900.7 1.7 fusion.254
  904.3 1.6 multiply_reduce_fusion.11
  907.9 1.7 fusion.254
  911.5 1.6 multiply_reduce_fusion.11
  915.2 1.7 fusion.254
  918.7 1.6 multiply_reduce_fusion.11
  922.4 1.7 fusion.254
  926.0 1.6 multiply_reduce_fusion.11
  929.6 1.7 fusion.254
  933.2 1.6 multiply_reduce_fusion.11
  936.8 1.7 fusion.254
  944.3 1.8 broadcast_select_fusion.1
  949.3 2.9 gather_fusion.3
  952.2 1.9 select_bitcast_fusion
  954.1 5.2 all_to_all.63
  960.3 4.6 convolution_bitcast_fusion.2
  964.9 18.2 copy.277
  983.2 12.1 reshape.544
  995.2 4.2 fusion.122
  999.4 8.2 reshape.541
  1007.6 8.5 copy.278
  1016.1 11.4 reshape.543
  1027.5 9.8 copy.279
  1037.4 30.1 %pad_maximum_fusion = f32[128,55296]{0,1:T(8,128)} fusion(f32[128,18432]{0,1:T(8,128)} %reshape.544, f32[128,18432]{0,1:T(8,128)} %copy.279, f32[128,4608]{0,1:T(8,128)S(1)} %copy-done.3, f32[128,13824]{0,1:T(8,128)} %copy.278), kind=kLoop, calls=%fused_computation.117 | loop fusion | flops 21233664 | bytes 56623104 | tf_op jit(solution)/shard_map/concatenate | solution.py:319
  1067.4 27.7 %copy.280 = f32[128,55296]{1,0:T(8,128)} copy(f32[128,55296]{0,1:T(8,128)} %pad_maximum_fusion) | data formatting | bytes 56623104 | tf_op jit(solution)/shard_map/concatenate | solution.py:319
  1095.2 25.1 %reshape.545 = f32[1024,6912]{1,0:T(8,128)} reshape(f32[128,55296]{1,0:T(8,128)} %copy.280) | data formatting | bytes 56623104 | tf_op jit(solution)/shard_map/reshape | solution.py:321
  1121.5 4.2 fusion.116
  1126.0 572.5 %all-reduce.4 = bf16[128,42]{1,0:T(8,128)(2,1)S(1)} all-reduce(f32[128,42]{1,0:T(8,128)S(1)} %pad_maximum_fusion.7), channel_id=2, replica_groups=mesh['seq'=2,'fsdp'=128] {'fsdp'}, use_global_device_ids=true, to_apply=%region_29.32.clone | all-reduce | flops 5376 | bytes 32256
  1699.2 112.9 %psum.14 = bf16[1,42]{1,0:T(2,128)(2,1)S(1)} all-reduce(bf16[1,42]{1,0:T(2,128)(2,1)S(1)} %dynamic-slice_convert_fusion), channel_id=1, replica_groups=mesh['seq'=2,'fsdp'=128] {'seq'}, use_global_device_ids=true, to_apply=%region_30.33 | all-reduce | flops 42 | bytes 168 | tf_op jit(solution)/shard_map/psum | solution.py:337
  1812.8 2.3 fusion.115
  1815.1 6.1 fusion.102
  1821.2 152.9 %reduce-scatter.2.cloned.1.call-done = f32[8,6912]{1,0:T(8,128)} async-done(((f32[1024,6912]{1,0:T(8,128)}), f32[8,6912]{1,0:T(8,128)}) %reduce-scatter.2.cloned.1.call-update) | async-done | bytes 221200 | tf_op jit(solution)/shard_map/reduce_scatter | solution.py:332
  1974.1 1.6 convert_element_type.170
  1976.3 32.2 %all-reduce.8.cloned.1.call-done = bf16[8,6912]{1,0:T(8,128)(2,1)} async-done(((bf16[8,6912]{1,0:T(8,128)(2,1)}), bf16[8,6912]{1,0:T(8,128)(2,1)}) %all-reduce.8.cloned.1.call-update) | async-done | bytes 110608 | tf_op jit(solution)/shard_map/psum | solution.py:336
  2008.5 7.9 slice.297
  (406 shorter events, 141.6 us)
Async XLA Ops:
  7.2 610.2 %all-gather.11.cloned.1.call-start = ((), (), s32[]{:S(2)}) async-start(), calls=%async_computation.8 | async-start | bytes 1585152 | tf_op jit(solution)/shard_map/all_gather | solution.py:145
  7.9 611.8 %all-gather.9.cloned.1.call-start = ((), (), s32[]{:S(2)}) async-start(), calls=%async_computation.7 | async-start | bytes 4755456 | tf_op jit(solution)/shard_map/all_gather | solution.py:144
  8.7 805.1 %all-gather.13.cloned.1.call-start = ((), (), s32[]{:S(2)}) async-start(), calls=%async_computation.9 | async-start | bytes 6340608 | tf_op jit(solution)/shard_map/all_gather | solution.py:147
  9.4 817.5 %all-gather.15.cloned.1.call-start = ((), (), s32[]{:S(2)}) async-start(), calls=%async_computation.10 | async-start | bytes 6340608 | tf_op jit(solution)/shard_map/all_gather | solution.py:149
  10.0 1964.1 %reduce-scatter.2.cloned.1.call-start = ((), (), s32[]{:S(2)}) async-start(), calls=%async_computation.5 | async-start | bytes 28532736 | tf_op jit(solution)/shard_map/reduce_scatter | solution.py:332
  10.0 15.9 copy-start.54
  12.8 15.7 copy-start.45
  13.5 741.9 %copy-start.40 = (pred[512]{0:T(512)(128)(4,1)}, pred[512]{0:T(512)(128)(4,1)S(1)}, u32[]{:S(2)}) copy-start(pred[512]{0:T(512)(128)(4,1)S(1)} %compare_and_fusion.1) | copy-start | bytes 1540
  24.1 602.2 %copy-start.30 = (f32[256]{0:T(256)}, f32[256]{0:T(256)S(1)}, u32[]{:S(2)}) copy-start(f32[256]{0:T(256)S(1)} %add_rsqrt_fusion.1) | copy-start | bytes 3076
  25.4 590.1 %copy-start.47 = (s32[256]{0:T(256)}, s32[256]{0:T(256)S(1)}, u32[]{:S(2)}) copy-start(s32[256]{0:T(256)S(1)} %get-tuple-element.1630) | copy-start | bytes 3076
  616.5 134.2 %copy-start.35 = (s32[1024]{0:T(1024)}, s32[1024]{0:T(1024)S(1)}, u32[]{:S(2)}) copy-start(s32[1024]{0:T(1024)S(1)} %get-tuple-element.1024) | copy-start | bytes 12292
  616.5 187.8 %copy-start.33 = (s32[1024]{0:T(1024)}, s32[1024]{0:T(1024)S(1)}, u32[]{:S(2)}) copy-start(s32[1024]{0:T(1024)S(1)} %get-tuple-element.1023) | copy-start | bytes 12292
  619.7 6.7 copy-start.2
  772.2 12.9 copy-start.50
  772.2 12.9 copy-start.52
  772.2 12.9 copy-start.55
  772.2 13.0 copy-start.58
  772.2 13.0 copy-start.60
  772.2 13.0 copy-start.64
  802.4 1.7 copy-start.10
  802.4 5.4 copy-start.22
  802.4 3.9 copy-start.42
  813.4 38.3 %copy-start = (f32[256,768]{1,0:T(8,128)}, f32[256,768]{1,0:T(8,128)S(1)}, u32[]{:S(2)}) copy-start(f32[256,768]{1,0:T(8,128)S(1)} %get-tuple-element.1018) | copy-start | bytes 2359300
  813.7 32.9 %copy-start.37 = (f32[256]{0:T(256)}, f32[256]{0:T(256)S(1)}, u32[]{:S(2)}) copy-start(f32[256]{0:T(256)S(1)} %add_rsqrt_fusion) | copy-start | bytes 3076
  813.7 7.8 copy-start.39
  826.9 7.8 copy-start.13
  846.5 5.1 copy-start.14
  854.0 7.8 copy-start.4
  854.0 1.3 copy-start.15
  854.0 5.9 copy-start.36
  854.5 7.4 copy-start.41
  859.9 2.5 copy-start.46
  859.9 2.5 copy-start.48
  859.9 2.5 copy-start.62
  859.9 2.5 copy-start.63
  862.4 32.6 %copy-start.51 = (s32[512]{0:T(512)S(1)}, s32[512]{0:T(512)}, u32[]{:S(2)}) copy-start(s32[512]{0:T(512)} %pad_add_fusion.1) | copy-start | bytes 6148
  862.4 32.6 %copy-start.53 = (s32[512]{0:T(512)S(1)}, s32[512]{0:T(512)}, u32[]{:S(2)}) copy-start(s32[512]{0:T(512)} %pad_add_fusion) | copy-start | bytes 6148
  862.4 32.6 %copy-start.56 = (pred[512]{0:T(512)(128)(4,1)S(1)}, pred[512]{0:T(512)(128)(4,1)}, u32[]{:S(2)}) copy-start(pred[512]{0:T(512)(128)(4,1)} %copy-done.54) | copy-start | bytes 1540
  862.4 32.6 %copy-start.59 = (pred[256]{0:T(512)(128)(4,1)S(1)}, pred[256]{0:T(512)(128)(4,1)}, u32[]{:S(2)}) copy-start(pred[256]{0:T(512)(128)(4,1)} %get-tuple-element.1584) | copy-start | bytes 772
  862.4 32.6 %copy-start.61 = (pred[256]{0:T(512)(128)(4,1)S(1)}, pred[256]{0:T(512)(128)(4,1)}, u32[]{:S(2)}) copy-start(pred[256]{0:T(512)(128)(4,1)} %get-tuple-element.1582) | copy-start | bytes 772
  862.5 32.6 %copy-start.65 = (pred[512]{0:T(512)(128)(4,1)S(1)}, pred[512]{0:T(512)(128)(4,1)}, u32[]{:S(2)}) copy-start(pred[512]{0:T(512)(128)(4,1)} %fusion.145) | copy-start | bytes 1540
  894.2 1.0 copy-start.20
  941.5 1.6 copy-start.57
  943.0 3.2 copy-start.9
  944.3 2.1 copy-start.11
  944.3 2.1 copy-start.17
  944.3 2.1 copy-start.6
  946.1 1.0 copy-start.21
  946.1 1.1 copy-start.19
  946.2 1.2 copy-start.26
  946.2 1.2 copy-start.27
  947.7 1.6 copy-start.34
  947.9 4.3 copy-start.43
  959.3 1.0 copy-start.12
  960.3 34.9 %copy-start.7 = (bf16[256,3,2,1,384]{0,4,2,1,3:T(8,128)(2,1)}, bf16[256,3,2,1,384]{0,4,2,1,3:T(8,128)(2,1)S(1)}, u32[]{:S(2)}) copy-start(bf16[256,3,2,1,384]{0,4,2,1,3:T(8,128)(2,1)S(1)} %copy.270) | copy-start | bytes 3538948
  983.1 12.1 copy-start.31
  1027.5 9.8 copy-start.3
  1120.2 0.9 copy-start.32
  1120.2 1.3 copy-start.8
  1120.3 888.2 %all-reduce.8.cloned.1.call-start = ((), (), s32[]{:S(2)}) async-start(), calls=%async_computation.6 | async-start | bytes 221184 | tf_op jit(solution)/shard_map/psum | solution.py:336
  1121.5 691.2 %copy-start.5 = (f32[256,768]{1,0:T(8,128)S(1)}, f32[256,768]{1,0:T(8,128)}, u32[]{:S(2)}) copy-start(f32[256,768]{1,0:T(8,128)} %copy-done.4) | copy-start | bytes 2359300
  1125.7 689.3 %copy-start.1 = (f32[256,768]{1,0:T(8,128)S(1)}, f32[256,768]{1,0:T(8,128)}, u32[]{:S(2)}) copy-start(f32[256,768]{1,0:T(8,128)} %copy-done) | copy-start | bytes 2359300
  2016.4 2.4 slice-start.1
  2016.4 3.5 slice-start
  (10 other events, 7.7 us)
Sparse Core Ops, SparseCore 0:
  11.4 103.6 all-gather.10
  118.8 116.9 all-gather.8
  239.5 116.9 all-gather.12
  359.9 116.4 all-gather.14
  1120.4 853.6 reduce-scatter.1
  1976.5 31.9 all-reduce.7
where the time goes:
time: 2040 us; the launch traced here: 2030 us
  blocking collectives  1400 us (69%)
  local copies, waits for them, and re-layouts  219 us (11%)
  waiting for transfers between devices  188 us (9%)
  matrix products  139 us (7%)
  other arithmetic  65.7 us (3%)
    unnamed x2, blocking collectives  1160 us
    reduce_scatter x1, waiting for transfers between devices, per_device(): lax.psum_scatter(matrix_pack, 'fsdp', scatter_dimension=0, tiled=True)  153 us
    all_to_all x1, blocking collectives, per_device(): lax.all_to_all(qkv_rows.reshape(row_count, 3, seq_count, head_cols), 'seq...  115 us
    psum x1, blocking collectives, per_device(): lax.psum(owned[1].astype(jnp.bfloat16), 'seq').astype(jnp.float32)  113 us
    unnamed x158, local copies, waits for them, and re-layouts  44 us
  transfers between devices with their start and end apart: 6, of which 2 were waited for; matrix products, arithmetic and copies ran while one was open for 6% of the time, Pallas kernels for 0%

commit v1 on v0

v1 whole, which is shorter than its diff:
```python
import jax
import jax.numpy as jnp
import numpy as np
from jax import lax
from jax.experimental import pallas as pl
from jax.experimental.pallas import tpu as pltpu
from jax.sharding import PartitionSpec as P

MESH = pl.DeviceIdType.MESH
BF = jnp.bfloat16
F32 = jnp.float32
EPS = 1e-05
NEG = -1e30

NT = 37
VEC, QKV, OUT, UP, DOWN = 0, list(range(1, 10)), [10, 11, 12], list(range(13, 25)), list(range(25, 37))
GVEC, GQKV, GOUT, GUP, GDOWN = 24, list(range(28, 37)), [25, 26, 27], list(range(12, 24)), list(range(12))


class Split:
    def __init__(self, ny, nx, nz, direct_z, direct_x, direct_wide):
        self.ny, self.nx, self.nz = ny, nx, nz
        self.direct_z, self.direct_x, self.direct_wide = direct_z, direct_x, direct_wide
        self.stages = range(len(ny))
        self.first = [sum(4 * ny[i] + nx[i] + nz[i] for i in range(st)) for st in self.stages]
        self.slab = [ny[i] + nx[i] + nz[i] for i in self.stages]

    def x(self, st):
        a = self.first[st] + 4 * self.ny[st]
        return a, a + self.nx[st]

    def z(self, st):
        a = self.first[st] + 4 * self.ny[st] + self.nx[st]
        return a, a + self.nz[st]

    def y(self, st, j):
        return pl.ds(self.first[st] + j * self.ny[st], self.ny[st])

    def tile(self, st, i, y):
        if i < self.ny[st]:
            return self.first[st] + y * self.ny[st] + i
        return self.first[st] + 3 * self.ny[st] + i


GATHER = Split((1, 2), (5, 8), (4, 8), (0, 0), (1, 1), (0, 0))
REDUCE = Split((2, 1), (9, 4), (8, 4), (0, 0), (1, 1), (0, 0))


class Place:
    pass


def chip(x, z, y):
    return x * 32 + z * 4 + y


def place():
    c = Place()
    c.f = lax.axis_index("fsdp")
    c.s = lax.axis_index("seq")
    c.x = c.f // 32
    c.z = (c.f // 4) % 8
    c.y = c.f % 4
    c.zh = c.z // 2
    c.zl = c.z % 2
    c.m = c.f % 8
    sgn = 2 * c.zl - 1
    c.xr = chip((c.x + 1) % 4, c.z, c.y)
    c.xl = chip((c.x + 3) % 4, c.z, c.y)
    c.xo = chip((c.x + 2) % 4, c.z, c.y)
    c.yo = chip(c.x, c.z, (c.y + 2) % 4)
    c.yr = chip(c.x, c.z, (c.y + 1) % 4)
    c.yl = chip(c.x, c.z, (c.y + 3) % 4)
    c.zo = chip(c.x, (c.z + 8 + sgn) % 8, c.y)
    c.zi = chip(c.x, (c.z + 8 - sgn) % 8, c.y)
    c.z2 = chip(c.x, (c.z + 8 + 2 * sgn) % 8, c.y)
    c.z2i = chip(c.x, (c.z + 8 - 2 * sgn) % 8, c.y)
    c.z3 = chip(c.x, (c.z + 8 + 3 * sgn) % 8, c.y)
    c.ke = (c.zh + 4 + sgn) % 4
    c.kf = (c.zh + 4 - sgn) % 4
    c.kp = (c.zh + 2) % 4
    return c


def greet(c):
    sem = pltpu.get_barrier_semaphore()
    group = [c.f - c.m + (c.m + d) % 8 for d in range(1, 8)]
    devices = [c.xr, c.xl, c.xo, c.zo, c.z2, c.z2i, c.z3] + group
    for d in devices:
        pl.semaphore_signal(sem, inc=1, device_id={"fsdp": d}, device_id_type=MESH)
    pl.semaphore_signal(sem, inc=1, device_id={"seq": 1 - c.s}, device_id_type=MESH)
    return len(devices) + 1


class Wires:
    def __init__(self, c, send_sem, recv_sem):
        self.c, self.send_sem, self.recv_sem = c, send_sem, recv_sem
        self.used, self.pending = 0, []

    def take(self, n):
        self.used += n
        return self.used - n

    def copy(self, src, dst, i, to):
        return pltpu.make_async_remote_copy(
            src_ref=src,
            dst_ref=dst,
            send_sem=self.send_sem.at[i],
            recv_sem=self.recv_sem.at[i],
            device_id=to,
            device_id_type=MESH,
        )

    def send(self, src, dst, i, to):
        to = to if isinstance(to, dict) else {"fsdp": to}
        d = self.copy(src, dst, i, to)
        d.start()
        self.pending.append(d)

    def wait(self, dst, i):
        self.copy(dst, dst, i, {"fsdp": self.c.f}).wait_recv()

    def finish(self):
        for d in self.pending:
            d.wait_send()


def gather_ring(w, block, halves, right, left, far, me, direct):
    i0 = w.take(4)
    bl, br, bo = (me + 3) % 4, (me + 1) % 4, (me + 2) % 4

    def send_all():
        for i, to in enumerate((right, left, far)):
            w.send(block(me), block(me), i0 + i, to)

    def wait_all():
        for i, k in enumerate((bl, br, bo)):
            w.wait(block(k), i0 + i)

    if direct:
        return [send_all, wait_all]

    def first():
        w.send(block(me), block(me), i0, right)
        w.send(block(me), block(me), i0 + 1, left)

    def second():
        w.wait(block(bl), i0)
        a = halves(bl)[0]
        w.send(a, a, i0 + 2, right)
        w.wait(block(br), i0 + 1)
        b = halves(br)[1]
        w.send(b, b, i0 + 3, left)

    def third():
        a, b = halves(bo)
        w.wait(a, i0 + 2)
        w.wait(b, i0 + 3)

    return [first, second, third]


def gather_pairs(w, half):
    c = w.c
    i0 = w.take(6)
    me, other = c.zl, 1 - c.zl

    def move(k, h, i, to):
        w.send(half(k, h), half(k, h), i0 + i, to)

    def got(k, h, i):
        w.wait(half(k, h), i0 + i)

    def s0():
        move(c.zh, other, 0, c.zo)

    def s1():
        got(c.ke, me, 0)
        move(c.ke, me, 2, c.zi)
        move(c.zh, me, 1, c.zo)

    def s2():
        got(c.kf, other, 2)
        move(c.kf, other, 4, c.zo)

    def s3():
        got(c.ke, other, 1)
        move(c.ke, other, 3, c.zi)

    def s4():
        got(c.kp, me, 4)
        move(c.kp, me, 5, c.zi)

    def s5():
        got(c.kf, me, 3)
        got(c.kp, other, 5)

    return [s0, s1, s2, s3, s4, s5]


def gather_relay(w, block, direct):
    c = w.c
    i0 = w.take(3)

    def send_all():
        for i, to in enumerate((c.zo, c.z2, c.z3)):
            w.send(block(c.zh), block(c.zh), i0 + i, to)

    def wait_all():
        for i, k in enumerate((c.ke, c.kf, c.kp)):
            w.wait(block(k), i0 + i)

    if direct:
        return [send_all, wait_all]

    def s0():
        w.send(block(c.zh), block(c.zh), i0, c.zo)

    def s1():
        w.wait(block(c.ke), i0)
        w.send(block(c.ke), block(c.ke), i0 + 1, c.zi)

    def s2():
        w.wait(block(c.kf), i0 + 1)
        w.send(block(c.kf), block(c.kf), i0 + 2, c.zo)

    def s3():
        w.wait(block(c.kp), i0 + 2)

    return [s0, s1, s2, s3]


def chain(*parts):
    steps = list(parts[0])
    for part in parts[1:]:
        last, then = steps.pop(), part[0]

        def both(last=last, then=then):
            last()
            then()

        steps += [both, *part[1:]]
    return steps


def named(events, name, steps):
    for i, fn in enumerate(steps):
        events[f"{name}{i}"] = fn


def gather_events(c, w, r):
    W, events = r.W, {}

    def stage(st):
        base = w.take(7)
        slab, held = getattr(r, f"gs{st}"), getattr(r, f"gh{st}")

        def start():
            for d in range(1, 8):
                dm = (c.m + d) % 8
                w.send(slab.at[dm % 4], held.at[c.m], base + d - 1, c.f - c.m + dm)
            held[c.m] = slab[c.y]

        def align():
            for d in range(1, 8):
                w.wait(held.at[(c.m + 8 - d) % 8], base + d - 1)
            row = lax.broadcasted_iota(jnp.int32, (48, 64), 0)
            col = lax.broadcasted_iota(jnp.int32, (48, 64), 1)
            pick = ((row // 6 == col // 8) & (row % 6 == col % 8)).astype(BF)
            for i in range(GATHER.slab[st]):
                v = held[:, i].reshape(64, 128)
                W[GATHER.tile(st, i, c.y), c.x, c.zh] = dot(pick, v).astype(BF)

        events[f"g{st}s"], events[f"g{st}a"] = start, align
        dz, dx, dw = GATHER.direct_z[st], GATHER.direct_x[st], GATHER.direct_wide[st]
        xa, xb = GATHER.x(st)
        za, zb = GATHER.z(st)
        zm = (za + zb + 1) // 2
        x = chain(
            gather_relay(w, lambda k: W.at[xa:xb, c.x, k], dz),
            gather_ring(
                w,
                lambda i: W.at[xa:xb, i],
                lambda i: (W.at[xa:xb, i, 0:2], W.at[xa:xb, i, 2:4]),
                c.xr,
                c.xl,
                c.xo,
                c.x,
                dw,
            ),
        )
        z = chain(
            gather_ring(
                w,
                lambda i: W.at[za:zb, i, c.zh],
                lambda i: (W.at[za:zm, i, c.zh], W.at[zm:zb, i, c.zh]),
                c.xr,
                c.xl,
                c.xo,
                c.x,
                dx,
            ),
            gather_pairs(w, lambda k, h: W.at[za:zb, pl.ds(2 * h, 2), k]),
        )
        mine = GATHER.y(st, c.y)
        y = chain(
            gather_relay(w, lambda k: W.at[mine, c.x, k], True),
            gather_ring(
                w,
                lambda i: W.at[mine, i],
                lambda i: (W.at[mine, i, 0:2], W.at[mine, i, 2:4]),
                c.xr,
                c.xl,
                c.xo,
                c.x,
                True,
            ),
            gather_ring(
                w,
                lambda i: W.at[GATHER.y(st, i)],
                lambda i: (W.at[GATHER.y(st, i), 0:2], W.at[GATHER.y(st, i), 2:4]),
                c.yr,
                c.yl,
                c.yo,
                c.y,
                dw,
            ),
        )
        named(events, f"g{st}x", x)
        named(events, f"g{st}y", y)
        named(events, f"g{st}z", z)

    for st in GATHER.stages:
        stage(st)
    return events


def gather_buffers():
    out = {}
    for st in GATHER.stages:
        out[f"gs{st}"] = ((4, GATHER.slab[st], 8, 128), BF)
        out[f"gh{st}"] = ((8, GATHER.slab[st], 8, 128), BF)
    return out


def fill_slab(c, r):
    zero = jnp.zeros((2, 128), BF)

    def vectors():
        lane = lax.broadcasted_iota(jnp.int32, (6, 128), 1)
        row = lax.broadcasted_iota(jnp.int32, (6, 128), 0)
        values = jnp.broadcast_to(r.vec[...].astype(F32), (6, 128))
        total = jnp.zeros((6, 128), F32)
        for col, at in [(0, row), (1, row + 6), (2, row + 12)] + [(4 + k, 18 + 4 * row + k) for k in range(4)]:
            v = jnp.sum(jnp.where(lane == at, values, 0.0), axis=1, keepdims=True)
            total = jnp.where(lane == col, v, total)
        return total.astype(BF)

    def tile(n):
        if n == VEC:
            return vectors()
        if n < 10:
            part, i = (n - 1) // 3, (n - 1) % 3
            return r.qkv[:, pl.ds(pl.multiple_of(part * 768 + c.s * 384 + i * 128, 128), 128)]
        if n < 13:
            return r.out[:, pl.ds(pl.multiple_of(c.s * 384 + (n - 10) * 128, 128), 128)]
        ref, i = (r.up, n - 13) if n < 25 else (r.down, n - 25)
        return ref[:, pl.ds(pl.multiple_of(c.s * 1536 + i * 128, 128), 128)]

    for st in GATHER.stages:
        slab = getattr(r, f"gs{st}")
        for i in range(GATHER.slab[st]):
            for j in range(4):
                if i < GATHER.ny[st] or j == 0:
                    v = tile(GATHER.tile(st, i, j))
                slab[j, i, 0:6] = v
                slab[j, i, 6:8] = zero


def rows_loop(fn, size=64):
    def body(i, carry):
        fn(pl.ds(pl.multiple_of(i * size, size), size))
        return carry

    lax.fori_loop(0, 512 // size, body, 0)


def dot(a, b):
    return jnp.dot(a, b, preferred_element_type=F32)


def dot_nt(a, b):
    return lax.dot_general(a, b, (((1,), (1,)), ((), ())), preferred_element_type=F32)


def dot_tn(a, b):
    return lax.dot_general(a, b, (((0,), (0,)), ((), ())), preferred_element_type=F32)


def wide(W, tiles, rows=None):
    parts = []
    for t in tiles:
        v = W[t].reshape(768, 128)
        parts.append(v if rows is None else v[rows[0] : rows[1]])
    return parts[0] if len(parts) == 1 else jnp.concatenate(parts, axis=1)


def pairs_of(tiles):
    return [(i, tiles[i : i + 2]) for i in range(0, len(tiles), 2)]


def partner_lanes(v):
    lane = lax.broadcasted_iota(jnp.int32, v.shape, 1) % 64
    return jnp.where(lane < 32, pltpu.roll(v, 96, 1), pltpu.roll(v, 32, 1))


def mean_of(v):
    return jnp.sum(v, axis=1, keepdims=True) * (1.0 / 768.0)


BLOCKS = ((0, 128, 0), (128, 256, 128), (256, 128, None), (384, 256, None))


class Held:
    pass


def layer_steps(c, w, r):
    s = c.s
    other = {"seq": 1 - s}
    own = pl.ds(pl.multiple_of(s * 256, 256), 256)
    oth = pl.ds(pl.multiple_of(256 - s * 256, 256), 256)
    i0 = w.take(6)
    W, G = r.W, r.G
    r.gm, r.gmb, r.ln2 = r.x, r.hid, r.dgiven
    r.dq, r.dk, r.dv = r.dgelu.at[0:2], r.dgelu.at[2:4], r.dgelu.at[4:6]
    steps = {}

    def step(fn):
        name = fn.__name__
        steps[f"{name}{sum(k.rstrip('0123456789') == name for k in steps)}"] = fn

    @step
    def exchange_rows():
        w.send(r.hidden, r.hid.at[own], i0, other)
        w.send(r.d_out, r.dgiven.at[own], i0 + 1, other)
        r.hid[own] = r.hidden[...]
        r.dgiven[own] = r.d_out[...]

    @step
    def tables():
        src = r.source[...]
        r.perm[...] = (lax.broadcasted_iota(jnp.int32, (512, 512), 0) == src).astype(BF)
        first_len = r.lengths[0, 0] * 16
        token = lax.broadcasted_iota(jnp.int32, (256, 256), 0)
        offset = jnp.where(token >= first_len, token - first_len, token)
        at_pos = (lax.broadcasted_iota(jnp.int32, (256, 256), 1) == offset).astype(BF)
        parts = dot(at_pos, r.table[...])
        cos_v = parts[:, 0:128] + parts[:, 128:256] + parts[:, 256:384]
        sin_v = parts[:, 384:512] + parts[:, 512:640] + parts[:, 640:768]
        r.cs[0:256], r.cs[256:512] = cos_v, cos_v
        r.sn[0:256], r.sn[256:512] = sin_v, sin_v
        row = lax.broadcasted_iota(jnp.int32, (512, 128), 0)
        lane = lax.broadcasted_iota(jnp.int32, (512, 128), 1)
        noisy = row < 256
        block = (row % 256) // 16
        first_blocks = r.lengths[0, 0]
        for h in range(2):
            col = lane - 64 * (1 - h)
            at = col % 16
            same = (block >= first_blocks) == (at >= first_blocks)
            clean_ok = same & ((at < block) | ((at == block) & ~noisy))
            ok = jnp.where(col < 16, clean_ok.astype(jnp.int32), (at == block).astype(jnp.int32))
            used = (col >= 0) & (col < 32)
            r.fq[h] = jnp.where(used & (ok == 0), NEG, 0.0).astype(BF)
            mine = jnp.where(noisy, block + 16, block)
            r.fk[h] = (used & (col == mine)).astype(BF)
        zero = jnp.zeros((128, 128), BF)
        for q in (0, 256):
            r.ds_c[0, q : q + 128, 128:256] = zero
            r.ds_c[1, q : q + 128, 128:256] = zero
            for head in range(6):
                r.ec[head, q : q + 128, 128:256] = zero

    @step
    def slot_order():
        w.wait(r.hid.at[oth], i0)
        for n in range(0, 768, 256):
            r.x[:, n : n + 256] = dot_tn(r.perm[...], r.hid[:, n : n + 256])

    @step
    def slot_order_grad():
        w.wait(r.dgiven.at[oth], i0 + 1)
        for n in range(0, 768, 256):
            r.dsl[:, n : n + 256] = dot_tn(r.perm[...], r.dgiven[:, n : n + 256]).astype(BF)
        r.dslT[...] = r.dsl[...].T
        r.grow[...] = jnp.sum(r.dsl[...].astype(F32), axis=0, keepdims=True)

    def norm(src_ref, n_ref, inv_ref, ln_ref, gain):
        def chunk(q):
            v = src_ref[q]
            cen = v - mean_of(v)
            inv = lax.rsqrt(mean_of(cen * cen) + EPS)
            nv = cen * inv
            n_ref[q] = nv
            inv_ref[q] = jnp.broadcast_to(inv, (64, 128))
            if ln_ref is not None:
                ln_ref[q] = (nv * r.vrow[gain : gain + 1]).astype(BF)

        rows_loop(chunk)

    @step
    def first_norm():
        norm(r.x, r.n1, r.inv1, None, 0)

    def ub_mask():
        d_of = lax.broadcasted_iota(jnp.int32, (384, 1536), 0)
        n_of = lax.broadcasted_iota(jnp.int32, (384, 1536), 1)
        spread = (
            lax.broadcasted_iota(jnp.int32, (128, 1536), 0)
            == 4 + lax.broadcasted_iota(jnp.int32, (128, 1536), 1) % 4
        ).astype(BF)
        return n_of // 4 == d_of, spread

    @step
    def vectors():
        r.vrow[...] = W[VEC].reshape(768, 128).astype(F32).T[0:8]

        def chunk(q):
            r.ln1[q] = (r.n1[q] * r.vrow[0:1]).astype(BF)

        rows_loop(chunk)

    first_all = lax.broadcasted_iota(jnp.int32, (512, 128), 1) < 64

    def qkv_step(i, tiles):
        def qkv():
            y = dot(r.ln1[...], wide(W, tiles))
            for k in range(len(tiles)):
                t = i + k
                v = y[:, 128 * k : 128 * k + 128].astype(BF)
                cols = slice(128 * (t % 3), 128 * (t % 3) + 128)
                if t >= 6:
                    one = jnp.ones_like(v)
                    r.v2[0, :, cols] = jnp.where(first_all, v, one)
                    r.v2[1, :, cols] = jnp.where(first_all, one, v)
                    continue
                f = v.astype(F32)
                f = (f * r.cs[...] + partner_lanes(f) * r.sn[...]).astype(BF)
                if t < 3:
                    f = f * 0.125
                to, fill = (r.q2, r.fq) if t < 3 else (r.k2, r.fk)
                to[0, :, cols] = jnp.where(first_all, f, fill[0])
                to[1, :, cols] = jnp.where(first_all, fill[1], f)

        return qkv

    for i, tiles in pairs_of(QKV):
        step(qkv_step(i, tiles))

    @step
    def up_bias():
        mask, spread = ub_mask()
        half_rows = W[VEC, pl.ds(2 * s, 2)].reshape(384, 128)
        r.ubrow[...] = jnp.sum(jnp.where(mask, dot(half_rows, spread), 0.0), axis=0, keepdims=True)

    lane = lax.broadcasted_iota(jnp.int32, (128, 128), 1)
    first = lane < 64

    def attend_step(p, blocks):
        def attend():
            cols = slice(128 * p, 128 * p + 128)
            items = [(slice(q0, q0 + 128), nc, k0, h) for q0, nc, k0 in blocks for h in range(2)]
            scores, outs = [], []
            for rows, nc, k0, h in items:
                q = r.q2[h, rows, cols]
                sc = dot_nt(q, r.k2[h, 256 : 256 + nc, cols])
                if k0 is not None:
                    sc = jnp.concatenate([sc, dot_nt(q, r.k2[h, k0 : k0 + 128, cols])], axis=1)
                scores.append(sc)
            tops = [jnp.max(sc, axis=1, keepdims=True) for sc in scores]
            exps = [jnp.exp(sc - top).astype(BF) for sc, top in zip(scores, tops)]
            for (rows, nc, k0, h), e in zip(items, exps):
                r.ec[2 * p + h, rows, 0:nc] = e[:, 0:nc]
                o = dot(e[:, 0:nc], r.v2[h, 256 : 256 + nc, cols])
                if k0 is not None:
                    r.en[2 * p + h, rows] = e[:, nc : nc + 128]
                    o = o + dot(e[:, nc : nc + 128], r.v2[h, k0 : k0 + 128, cols])
                outs.append(o)
            for i in range(0, len(items), 2):
                rows, one, two = items[i][0], outs[i], outs[i + 1]
                rec = 1.0 / jnp.where(first, pltpu.roll(one, 64, 1), pltpu.roll(two, 64, 1))
                r.rec[rows, cols] = rec
                r.att[rows, cols] = (jnp.where(first, one, two) * rec).astype(BF)

        return attend

    for p in range(3):
        step(attend_step(p, BLOCKS[:2]))
        step(attend_step(p, BLOCKS[2:]))

    @step
    def out_product():
        for n in range(0, 768, 256):
            y = dot_nt(r.att[...], wide(W, OUT, (n, n + 256)))
            r.part[:, n : n + 256] = y
            r.sendb[0, :, n : n + 256] = y.astype(BF)
        w.send(r.sendb.at[0], r.recvb.at[0], i0 + 2, other)

    @step
    def second_norm():
        w.wait(r.recvb.at[0], i0 + 2)

        def add_mid(q):
            r.middle[q] = r.x[q] + r.part[q] + r.recvb[0, q].astype(F32)

        rows_loop(add_mid)
        norm(r.middle, r.n2, r.inv2, r.ln2, 1)

    def up_step(i, tiles):
        def up():
            cols = slice(128 * i, 128 * i + 256)
            pre = dot(r.ln2[...], wide(W, tiles)) + r.ubrow[:, cols]
            sq = pre * pre
            th = jnp.tanh(0.7978845608028654 * (pre + 0.044715 * pre * sq))
            r.act[:, cols] = (0.5 * pre * (1.0 + th)).astype(BF)
            slope = 0.5 * (1.0 + th) + 0.5 * pre * (1.0 - th * th) * (
                0.7978845608028654 * (1.0 + 0.134145 * sq)
            )
            r.dgelu[i], r.dgelu[i + 1] = slope[:, 0:128], slope[:, 128:256]

        return up

    for i, tiles in pairs_of(UP):
        step(up_step(i, tiles))

    def store(tiles, y):
        for k, t in enumerate(tiles):
            G[t] = y[:, 128 * k : 128 * k + 128].astype(BF).reshape(4, 4, 48, 128)

    def weight_steps(name, tiles, leftT, right):
        def make(i, group):
            def fn():
                store(group, dot(leftT[...], right[:, 128 * i : 128 * (i + len(group))]))

            fn.__name__ = name
            return fn

        for i, group in pairs_of(tiles):
            step(make(i, group))

    weight_steps("grad_down", GDOWN, r.dslT, r.act)

    def down_back_step(i, tiles):
        def down_back():
            cols = slice(128 * i, 128 * i + 256)
            slope = jnp.concatenate([r.dgelu[i], r.dgelu[i + 1]], axis=1)
            g = (dot(r.dsl[...], wide(W, tiles)) * slope).astype(BF)
            r.gpre[:, cols] = g
            r.gub[:, cols] = jnp.sum(g.astype(F32), axis=0, keepdims=True)

        return down_back

    for i, tiles in pairs_of(DOWN):
        step(down_back_step(i, tiles))

    @step
    def up_back():
        for n in range(0, 768, 256):
            y = dot_nt(r.gpre[...], wide(W, UP, (n, n + 256)))
            r.part[:, n : n + 256] = y
            r.sendb[1, :, n : n + 256] = y.astype(BF)
        w.send(r.sendb.at[1], r.recvb.at[1], i0 + 3, other)

    @step
    def grad_vectors():
        rows = jnp.concatenate(
            [jnp.zeros((2, 768), F32), r.grow[...], jnp.zeros((125, 768), F32)], axis=0
        )
        G[GVEC] = rows.T.astype(BF).reshape(4, 4, 48, 128)
        mask, spread = ub_mask()
        ub = dot_nt(jnp.where(mask, r.gub[...], 0.0).astype(BF), spread)
        old = G[GVEC, pl.ds(2 * s, 2)].reshape(384, 128)
        G[GVEC, pl.ds(2 * s, 2)] = (old.astype(F32) + ub).astype(BF).reshape(2, 4, 48, 128)

    @step
    def lnb_t():
        r.lnbT[...] = r.ln2[...].T

    weight_steps("grad_up", GUP, r.lnbT, r.gpre)

    @step
    def middle_back():
        w.wait(r.recvb.at[1], i0 + 3)

        def mid_back(q):
            gl = r.part[q] + r.recvb[1, q].astype(F32)
            nv = r.n2[q]
            u = gl * r.vrow[1:2]
            g = r.dsl[q].astype(F32) + r.inv2[q][:, 0:1] * (u - mean_of(u) - nv * mean_of(u * nv))
            r.gm[q] = g
            r.gmb[q] = g.astype(BF)

        rows_loop(mid_back)

    @step
    def out_back():
        for i, tiles in pairs_of(OUT):
            r.gatt[:, 128 * i : 128 * (i + len(tiles))] = dot(r.gmb[...], wide(W, tiles)).astype(BF)

    @step
    def grad_out_t():
        r.gmT[...] = r.gmb[...].T

    weight_steps("grad_out", GOUT, r.gmT, r.att)

    def attend_prep_step(p):
        def attend_prep():
            cols = slice(128 * p, 128 * p + 128)
            ga = r.gatt[:, cols].astype(F32) * r.rec[:, cols]
            gb = ga.astype(BF)
            r.ga[:, cols] = gb
            t = gb.astype(F32) * r.att[:, cols].astype(F32)
            hi = t.astype(BF)
            lo = (t - hi.astype(F32)).astype(BF)
            li = lax.broadcasted_iota(jnp.int32, (128, 128), 0)
            lj = lax.broadcasted_iota(jnp.int32, (128, 128), 1)
            across = ((li < 64) != (lj < 64)).astype(BF)
            delta = -(dot(hi, across) + dot(lo, across))
            dh = delta.astype(BF)
            dl = (delta - dh.astype(F32)).astype(BF)
            ln = lax.broadcasted_iota(jnp.int32, (512, 128), 1) % 64
            fill = jnp.where(ln == 0, dh, jnp.where(ln == 1, dl, jnp.zeros_like(dh)))
            r.g2[0, :, cols] = jnp.where(first_all, gb, fill)
            r.g2[1, :, cols] = jnp.where(first_all, fill, gb)

        return attend_prep

    def attend_back_step(p, h):
        def attend_back():
            head = 2 * p + h
            cols = slice(128 * p, 128 * p + 128)
            items = [(slice(q0, q0 + 128), nc, k0) for q0, nc, k0 in BLOCKS]
            dps = []
            for rows, nc, k0 in items:
                g = r.g2[h, rows, cols]
                dp = dot_nt(g, r.v2[h, 256 : 256 + nc, cols])
                if k0 is not None:
                    dp = jnp.concatenate([dp, dot_nt(g, r.v2[h, k0 : k0 + 128, cols])], axis=1)
                dps.append(dp)
            ds = []
            for (rows, nc, k0), dp in zip(items, dps):
                e = r.ec[head, rows, 0:nc]
                if k0 is not None:
                    e = jnp.concatenate([e, r.en[head, rows]], axis=1)
                ds.append((e.astype(F32) * dp).astype(BF))
            for (rows, nc, k0), d in zip(items, ds):
                r.ds_c[h, rows, 0:nc] = d[:, 0:nc]
                o = dot(d[:, 0:nc], r.k2[h, 256 : 256 + nc, cols])
                if k0 is not None:
                    o = o + dot(d[:, nc : nc + 128], r.k2[h, k0 : k0 + 128, cols])
                    r.dk[h, rows] = dot_tn(d[:, nc : nc + 128], r.q2[h, rows, cols])
                    r.dv[h, rows] = dot_tn(r.en[head, rows], r.ga[rows, cols])
                r.dq[h, rows] = o
            r.dk[h, 256:512] = dot_tn(r.ds_c[h], r.q2[h, :, cols])
            r.dv[h, 256:512] = dot_tn(r.ec[head], r.ga[:, cols])

        return attend_back

    def attend_join_step(p):
        def attend_join():
            for i, (ref, scale) in enumerate(((r.dq, 0.125), (r.dk, 1.0))):
                v = jnp.where(first_all, ref[0], ref[1]) * scale
                v = v * r.cs[...] - partner_lanes(v) * r.sn[...]
                r.grows[:, 384 * i + 128 * p : 384 * i + 128 * p + 128] = v.astype(BF)
            v = jnp.where(first_all, r.dv[0], r.dv[1])
            r.grows[:, 768 + 128 * p : 768 + 128 * p + 128] = v.astype(BF)

        return attend_join

    for p in range(3):
        step(attend_prep_step(p))
        step(attend_back_step(p, 0))
        step(attend_back_step(p, 1))
        step(attend_join_step(p))

    @step
    def lna_t():
        r.lnaT[...] = r.ln1[...].T

    weight_steps("grad_qkv", GQKV, r.lnaT, r.grows)

    @step
    def qkv_back():
        for n in range(0, 768, 256):
            r.part[:, n : n + 256] = dot_nt(r.grows[...], wide(W, QKV, (n, n + 256)))

    @step
    def first_back():
        def chunk(q):
            gl = r.part[q]
            nv = r.n1[q]
            u = gl * r.vrow[0:1]
            r.part[q] = r.inv1[q][:, 0:1] * (u - mean_of(u) - nv * mean_of(u * nv))

        rows_loop(chunk)

    @step
    def hidden_other():
        r.half_out[0] = dot(r.perm[oth], r.part[...].astype(BF)).astype(BF)
        w.send(r.half_out.at[0], r.half_in.at[0], i0 + 4, other)

    def back_to_given(v):
        hi = v.astype(BF)
        lo = (v - hi.astype(F32)).astype(BF)
        return dot(r.perm[own], hi) + dot(r.perm[own], lo)

    @step
    def hidden_own():
        for n in range(0, 768, 256):
            r.grad_hidden[:, n : n + 256] = back_to_given(r.gm[:, n : n + 256] + r.part[:, n : n + 256])

    def down_product_step(n):
        def down_product():
            cols = slice(n, n + 256)
            y = dot_nt(r.act[...], wide(W, DOWN, (n, n + 256)))
            r.half_out[1, :, cols] = dot(r.perm[oth], y.astype(BF)).astype(BF)
            r.outp[:, cols] = back_to_given(y + r.middle[:, cols] + r.vrow[2:3, cols])
            if n == 512:
                w.send(r.half_out.at[1], r.half_in.at[1], i0 + 5, other)

        return down_product

    for n in (0, 256, 512):
        step(down_product_step(n))

    @step
    def outputs():
        w.wait(r.half_in.at[0], i0 + 4)
        r.grad_hidden[...] += r.half_in[0].astype(F32)
        w.wait(r.half_in.at[1], i0 + 5)
        r.output[...] = (r.outp[...] + r.half_in[1].astype(F32)).astype(BF)

    return steps


LAYER_BUFFERS = dict(
    hid=((512, 768), BF),
    dgiven=((512, 768), BF),
    perm=((512, 512), BF),
    x=((512, 768), F32),
    n1=((512, 768), F32),
    inv1=((512, 128), F32),
    ln1=((512, 768), BF),
    lnaT=((768, 512), BF),
    lnbT=((768, 512), BF),
    gmT=((768, 512), BF),
    dslT=((768, 512), BF),
    cs=((512, 128), F32),
    sn=((512, 128), F32),
    fq=((2, 512, 128), BF),
    fk=((2, 512, 128), BF),
    q2=((2, 512, 384), BF),
    k2=((2, 512, 384), BF),
    v2=((2, 512, 384), BF),
    ec=((6, 512, 256), BF),
    en=((6, 256, 128), BF),
    ds_c=((2, 512, 256), BF),
    rec=((512, 384), F32),
    ga=((512, 384), BF),
    g2=((2, 512, 384), BF),
    att=((512, 384), BF),
    part=((512, 768), F32),
    sendb=((2, 512, 768), BF),
    recvb=((2, 512, 768), BF),
    middle=((512, 768), F32),
    n2=((512, 768), F32),
    inv2=((512, 128), F32),
    act=((512, 1536), BF),
    dgelu=((12, 512, 128), F32),
    dsl=((512, 768), BF),
    gpre=((512, 1536), BF),
    gatt=((512, 384), BF),
    grows=((512, 1152), BF),
    outp=((256, 768), F32),
    half_in=((2, 256, 768), BF),
    half_out=((2, 256, 768), BF),
    vrow=((8, 768), F32),
    grow=((1, 768), F32),
    ubrow=((1, 1536), F32),
    gub=((1, 1536), F32),
)


def add_to(dst, *terms):
    total = dst[...].astype(F32)
    for t in terms:
        total = total + t[...].astype(F32)
    dst[...] = total.astype(BF)


def reduce_ring(w, block, halves, got, far, right, left, over, me, whole, direct):
    i0 = w.take(6)
    bl, br, bo = (me + 3) % 4, (me + 1) % 4, (me + 2) % 4

    def send_all():
        for i, (k, to) in enumerate(((br, right), (bl, left), (bo, over))):
            w.send(block(k), whole[i], i0 + i, to)

    def wait_all():
        for i in range(3):
            w.wait(whole[i], i0 + i)
        add_to(block(me), *whole)

    if direct:
        return [send_all, wait_all]
    (la, lb), (ra, rb) = got
    fl, fr = far

    def first():
        a, b = halves(bo)
        w.send(a, fl, i0, right)
        w.send(b, fr, i0 + 1, left)
        w.send(halves(br)[1], lb, i0 + 2, right)
        w.send(halves(bl)[0], ra, i0 + 3, left)

    def second():
        w.wait(fl, i0)
        a = halves(br)[0]
        add_to(a, fl)
        w.send(a, la, i0 + 4, right)
        w.wait(fr, i0 + 1)
        b = halves(bl)[1]
        add_to(b, fr)
        w.send(b, rb, i0 + 5, left)

    def third():
        a, b = halves(me)
        w.wait(lb, i0 + 2)
        w.wait(rb, i0 + 5)
        add_to(b, lb, rb)
        w.wait(ra, i0 + 3)
        w.wait(la, i0 + 4)
        add_to(a, la, ra)

    return [first, second, third]


def reduce_pairs(w, half, narrow, wide):
    c = w.c
    i0 = w.take(6)
    me, other = c.zl, 1 - c.zl

    def move(k, h, to, i, chip_id):
        w.send(half(k, h), to, i0 + i, chip_id)

    def got(k, h, ref, i):
        w.wait(ref, i0 + i)
        add_to(half(k, h), ref)

    def s0():
        move(c.kp, other, narrow(0), 0, c.zi)

    def s1():
        got(c.kp, me, narrow(0), 0)
        move(c.kp, me, narrow(1), 2, c.zo)
        move(c.kf, me, wide(0, me), 1, c.zi)

    def s2():
        got(c.kf, other, narrow(1), 2)
        move(c.kf, other, wide(0, other), 4, c.zi)

    def s3():
        got(c.ke, other, wide(0, other), 1)
        move(c.ke, other, wide(1, other), 3, c.zo)

    def s4():
        got(c.ke, me, wide(0, me), 4)
        move(c.ke, me, wide(1, me), 5, c.zo)

    def s5():
        got(c.zh, me, wide(1, me), 3)
        got(c.zh, other, wide(1, other), 5)

    return [s0, s1, s2, s3, s4, s5]


def reduce_relay(w, block, got, direct):
    c = w.c
    i0 = w.take(3)

    def send_all():
        for i, (k, to) in enumerate(((c.ke, c.zo), (c.kf, c.z2i), (c.kp, c.z3))):
            w.send(block(k), got[i], i0 + i, to)

    def wait_all():
        for i in range(3):
            w.wait(got[i], i0 + i)
        add_to(block(c.zh), *got)

    if direct:
        return [send_all, wait_all]

    def s0():
        w.send(block(c.kp), got[0], i0, c.zo)

    def s1():
        w.wait(got[0], i0)
        add_to(block(c.kf), got[0])
        w.send(block(c.kf), got[1], i0 + 1, c.zi)

    def s2():
        w.wait(got[1], i0 + 1)
        add_to(block(c.ke), got[1])
        w.send(block(c.ke), got[2], i0 + 2, c.zo)

    def s3():
        w.wait(got[2], i0 + 2)
        add_to(block(c.zh), got[2])

    return [s0, s1, s2, s3]


def reduce_events(c, w, r):
    G, events = r.G, {}

    def stage(st):
        dz, dx, dw = REDUCE.direct_z[st], REDUCE.direct_x[st], REDUCE.direct_wide[st]
        xa, xb = REDUCE.x(st)
        za, zb = REDUCE.z(st)
        nz = zb - za
        zm = (nz + 1) // 2

        def buf(name):
            return getattr(r, f"r{st}{name}")

        def sides(ref, cut):
            return [(ref.at[(i, slice(None), slice(0, cut))], ref.at[(i, slice(None), slice(cut, 2 * cut))]) for i in range(2)]

        bx, bxf, bxz = buf("x"), buf("xf"), buf("xz")
        x = chain(
            reduce_ring(
                w,
                lambda i: G.at[xa:xb, i],
                lambda i: (G.at[xa:xb, i, 0:2], G.at[xa:xb, i, 2:4]),
                sides(bx, 2),
                (bxf.at[0], bxf.at[1]),
                c.xr,
                c.xl,
                c.xo,
                c.x,
                [bx.at[i] for i in range(3)] if dw else None,
                dw,
            ),
            reduce_relay(w, lambda k: G.at[xa:xb, c.x, k], [bxz.at[i] for i in range(3)], dz),
        )
        bz, bzh, bzx = buf("z"), buf("zh"), buf("zx")
        z = chain(
            reduce_pairs(
                w,
                lambda k, h: G.at[za:zb, pl.ds(2 * h, 2), k],
                lambda i: bzh.at[i],
                lambda i, h: bz.at[i, :, pl.ds(2 * h, 2)],
            ),
            reduce_ring(
                w,
                lambda i: G.at[za:zb, i, c.zh],
                lambda i: (G.at[za : za + zm, i, c.zh], G.at[za + zm : zb, i, c.zh]),
                [(bzx.at[i, 0:zm], bzx.at[i, zm:nz]) for i in range(2)],
                (bzx.at[2, 0:zm], bzx.at[2, zm:nz]),
                c.xr,
                c.xl,
                c.xo,
                c.x,
                [bzx.at[i] for i in range(3)] if dx else None,
                dx,
            ),
        )
        mine = REDUCE.y(st, c.y)
        by, byf, byx, byxf, byz = buf("y"), buf("yf"), buf("yx"), buf("yxf"), buf("yz")
        y = chain(
            reduce_ring(
                w,
                lambda i: G.at[REDUCE.y(st, i)],
                lambda i: (G.at[REDUCE.y(st, i), 0:2], G.at[REDUCE.y(st, i), 2:4]),
                sides(by, 2),
                (byf.at[0], byf.at[1]),
                c.yr,
                c.yl,
                c.yo,
                c.y,
                [by.at[i] for i in range(3)] if dw else None,
                dw,
            ),
            reduce_ring(
                w,
                lambda i: G.at[mine, i],
                lambda i: (G.at[mine, i, 0:2], G.at[mine, i, 2:4]),
                sides(byx, 2),
                (byxf.at[0], byxf.at[1]),
                c.xr,
                c.xl,
                c.xo,
                c.x,
                [byx.at[i] for i in range(3)],
                True,
            ),
            reduce_relay(w, lambda k: G.at[mine, c.x, k], [byz.at[i] for i in range(3)], True),
        )

        def group(name, a, b):
            base = w.take(7)
            slab, held = buf("s" + name), buf("h" + name)

            def spread():
                row = lax.broadcasted_iota(jnp.int32, (64, 48), 0)
                col = lax.broadcasted_iota(jnp.int32, (64, 48), 1)
                pick = ((col // 6 == row // 8) & (col % 6 == row % 8)).astype(BF)
                for i in range(a, b):
                    o = dot(pick, G[REDUCE.tile(st, i, c.y), c.x, c.zh]).astype(BF)
                    slab[:, i - a] = o.reshape(8, 8, 128)
                for d in range(1, 8):
                    dm = (c.m + d) % 8
                    w.send(slab.at[dm], held.at[c.m], base + d - 1, c.f - c.m + dm)
                held[c.m] = slab[c.m]

            def collect():
                for d in range(1, 8):
                    w.wait(held.at[(c.m + 8 - d) % 8], base + d - 1)
                for i in range(a, b):
                    v = held[:, i - a].astype(F32)
                    if i < REDUCE.ny[st]:
                        for j in range(4):
                            r.done[c.s, REDUCE.tile(st, i, j)] = v[j] + v[j + 4]
                    else:
                        r.done[c.s, REDUCE.tile(st, i, 0)] = jnp.sum(v, axis=0)

            return [spread, collect]

        ny, nx = REDUCE.ny[st], REDUCE.nx[st]
        named(events, f"r{st}y", chain(y, group("y", 0, ny)))
        named(events, f"r{st}x", chain(x, group("x", ny, ny + nx)))
        named(events, f"r{st}z", chain(z, group("z", ny + nx, ny + nx + nz)))
        i0 = w.take(1)
        tiles = slice(REDUCE.first[st], REDUCE.first[st] + 4 * ny + nx + nz)

        def share():
            w.send(r.done.at[c.s, tiles], r.done.at[c.s, tiles], i0, {"seq": 1 - c.s})

        def shared():
            w.wait(r.done.at[1 - c.s, tiles], i0)

        named(events, f"r{st}d", [share, shared])

    for st in REDUCE.stages:
        stage(st)
    return events


def reduce_buffers():
    out = {}
    for st in REDUCE.stages:
        ny, nx, nz = REDUCE.ny[st], REDUCE.nx[st], REDUCE.nz[st]
        for name, dims in dict(
            x=(2 + REDUCE.direct_wide[st], nx, 4, 48, 128),
            xf=(2, nx, 2, 48, 128),
            xz=(3, nx, 48, 128),
            z=(2, nz, 4, 48, 128),
            zh=(2, nz, 2, 48, 128),
            zx=(3, nz, 48, 128),
            y=(2 + REDUCE.direct_wide[st], ny, 4, 4, 48, 128),
            yf=(2, ny, 2, 4, 48, 128),
            yx=(3, ny, 4, 48, 128),
            yxf=(2, ny, 2, 48, 128),
            yz=(3, ny, 48, 128),
            sx=(8, nx, 8, 128),
            hx=(8, nx, 8, 128),
            sy=(8, ny, 8, 128),
            hy=(8, ny, 8, 128),
            sz=(8, nz, 8, 128),
            hz=(8, nz, 8, 128),
        ).items():
            out[f"r{st}{name}"] = (dims, BF)
    return out


def rotary_table():
    freq = np.power(np.float32(10000.0), -2.0 * np.arange(32, dtype=np.float32) / np.float32(64))
    angle = np.arange(256, dtype=np.float32)[:, None] * freq.astype(np.float32)[None, :]
    cos, sin = np.cos(angle).astype(np.float32), np.sin(angle).astype(np.float32)
    terms = []
    for v in (np.concatenate([cos] * 4, axis=1), np.concatenate([-sin, sin] * 2, axis=1)):
        for _ in range(3):
            low = v.astype(BF)
            terms.append(low)
            v = v - low.astype(np.float32)
    return np.concatenate(terms, axis=1)


SCHEDULE = (
    77, 0, 1, 2, 97, 78, 3, 85, 90, 79, 98, 91, 80, 86, 105, 110, 99, 81, 106, 82, 87, 92, 111, 100, 88, 93, 94, 107,
    101, 112, 89, 83, 95, 102, 84, 113, 96, 4, 5, 114, 108, 6, 7, 8, 9, 10, 11, 12, 13, 14, 15, 16, 17, 109, 63, 103,
    115, 18, 104, 39, 116, 19, 20, 21, 22, 23, 24, 25, 26, 27, 28, 29, 30, 31, 32, 33, 34, 35, 36, 37, 38, 40, 41,
    42, 43, 44, 45, 123, 117, 130, 73, 46, 47, 48, 49, 50, 51, 52, 53, 54, 55, 56, 131, 57, 58, 59, 60, 61, 62, 64,
    65, 66, 118, 67, 68, 140, 153, 146, 124, 132, 133, 69, 70, 71, 72, 74, 154, 75, 141, 134, 147, 119, 125, 155,
    156, 76, 142, 157, 148, 126, 120, 135, 143, 149, 127, 144, 150, 158, 121, 136, 128, 122, 151, 137, 145, 159, 152,
    129, 138, 160, 161, 139, 162,
)

INPUTS = ("hidden", "d_out", "lengths", "source", "table", "qkv", "out", "up", "down", "vec")
OUTPUTS = ("output", "grad_hidden", "done")
BUFFERS = {
    "W": ((NT, 4, 4, 48, 128), BF),
    "G": ((NT, 4, 4, 48, 128), BF),
    **LAYER_BUFFERS,
    **gather_buffers(),
    **reduce_buffers(),
}
SEMS = 6 + 35 * len(GATHER.stages) + 58 * len(REDUCE.stages)


def step_kernel(*refs):
    r = Held()
    for name, ref in zip(INPUTS + OUTPUTS + tuple(BUFFERS), refs):
        setattr(r, name, ref)
    c = place()
    w = Wires(c, refs[-2], refs[-1])
    greeted = greet(c)
    events = {**layer_steps(c, w, r), **gather_events(c, w, r), **reduce_events(c, w, r)}
    fill_slab(c, r)
    events.pop("tables0")()
    pl.semaphore_wait(pltpu.get_barrier_semaphore(), greeted)
    steps = list(events.values())
    assert sorted(SCHEDULE) == list(range(len(steps)))
    for i in SCHEDULE:
        steps[i]()
    w.finish()


def finish_kernel(
    out_in, hidden_in, done, qkv, up, vec, out, hidden, gqkv, gout, gup, gdown, g1, g2, gub, gdb
):
    out[...] = out_in[...]
    hidden[...] = hidden_in[...]
    for core in range(2):
        for i, t in enumerate(GQKV):
            n = (i // 3) * 768 + core * 384 + (i % 3) * 128
            gqkv[:, n : n + 128] = done[core, t, 0:6]
        for tiles, ref, half in ((GOUT, gout, 384), (GUP, gup, 1536), (GDOWN, gdown, 1536)):
            for i, t in enumerate(tiles):
                n = core * half + i * 128
                ref[:, n : n + 128] = done[core, t, 0:6]
    lane = lax.broadcasted_iota(jnp.int32, (6, 128), 1)
    row = lax.broadcasted_iota(jnp.int32, (6, 128), 0)
    one = done[0, GVEC, 0:6]
    both = one + done[1, GVEC, 0:6]
    values = jnp.broadcast_to(vec[...].astype(F32), (6, 128))

    def as_row(places):
        total = jnp.zeros((6, 128), F32)
        for v, at in places:
            total = jnp.where(lane == at, v, total)
        return jnp.sum(total, axis=0)

    def gain_grad(weight, grad, first):
        gain = jnp.sum(jnp.where(lane == row + first, values, 0.0), axis=1, keepdims=True)
        return jnp.sum(weight[...].astype(F32) * grad[...], axis=1, keepdims=True) / gain

    g1[...] = as_row([(gain_grad(qkv, gqkv, 0), row)])[0:6]
    g2[...] = as_row([(gain_grad(up, gup, 6), row)])[0:6]
    gdb[...] = as_row([(one[:, 2:3], row)])[0:6]
    gub[...] = as_row([(both[:, 4 + k : 5 + k], 4 * row + k) for k in range(4)])[0:24]


VM = pl.BlockSpec(memory_space=pltpu.VMEM)
LIMIT = 62 * 2**20


def shape(dims, dtype=F32):
    return jax.ShapeDtypeStruct(dims, dtype)


def per_device(
    hidden, d_out, lengths, slot_source, first_gain, qkv_weight, out_weight, second_gain, up_weight, up_bias,
    down_weight, down_bias,
):
    vec = jnp.concatenate([first_gain, second_gain, down_bias, up_bias, jnp.zeros((86,), BF)])[None]
    parts = pl.pallas_call(
        step_kernel,
        out_shape=(shape((256, 768), BF), shape((256, 768)), shape((2, NT, 8, 128))),
        in_specs=[VM, VM, pl.BlockSpec(memory_space=pltpu.SMEM)] + [VM] * 7,
        out_specs=(VM,) * 3,
        scratch_shapes=[pltpu.VMEM(*v) for v in BUFFERS.values()] + [pltpu.SemaphoreType.DMA((SEMS,))] * 2,
        compiler_params=pltpu.CompilerParams(collective_id=0, has_side_effects=True, vmem_limit_bytes=LIMIT),
    )(
        hidden[0], d_out[0], lengths, slot_source, rotary_table(),
        qkv_weight, out_weight.T, up_weight, down_weight.T, vec,
    )
    output, grad_hidden, gqkv, gout, gup, gdown, g1, g2, gub, gdb = pl.pallas_call(
        finish_kernel,
        out_shape=(
            shape((256, 768), BF),
            shape((256, 768)),
            shape((6, 2304)),
            shape((6, 768)),
            shape((6, 3072)),
            shape((6, 3072)),
            shape((6,)),
            shape((6,)),
            shape((24,)),
            shape((6,)),
        ),
        in_specs=[VM] * 6,
        out_specs=(VM,) * 10,
    )(*parts, qkv_weight, up_weight, vec)
    return (output[None], grad_hidden[None], g1, gqkv, gout.T, g2, gup, gub, gdown.T, gdb)


def solution(mesh):
    return jax.shard_map(
        per_device,
        mesh=mesh,
        in_specs=(
            P("fsdp", "seq", None),
            P("fsdp", "seq", None),
            P("fsdp", None),
            P("fsdp", None),
            P("fsdp"),
            P("fsdp", None),
            P(None, "fsdp"),
            P("fsdp"),
            P("fsdp", None),
            P("fsdp"),
            P(None, "fsdp"),
            P("fsdp"),
        ),
        out_specs=(
            P("fsdp", "seq", None),
            P("fsdp", "seq", None),
            P("fsdp"),
            P("fsdp", None),
            P(None, "fsdp"),
            P("fsdp"),
            P("fsdp", None),
            P("fsdp"),
            P(None, "fsdp"),
            P("fsdp"),
        ),
        check_vma=False,
    )
```

time: 2040 us -> 128 us (0.06)
  blocking collectives: 1400 us -> 0 us
  local copies, waits for them, and re-layouts: 219 us -> 1.34 us
  waiting for transfers between devices: 188 us -> 0 us
  matrix products: 139 us -> 0 us
  Pallas kernels: 0 us -> 125 us
  other arithmetic: 65.7 us -> 0 us
    unnamed x2 -> x0, blocking collectives: 1160 us -> none
    reduce_scatter x1 -> x0, waiting for transfers between devices: 153 us -> none  [per_device(): lax.psum_scatter(matrix_pack, 'fsdp', scatter_dimension=0, tiled=True)]
    dot_general x96 -> x0, matrix products: 139 us -> none  [the longest x12 16.8 us: head_backward(): jnp.einsum('qk,qd->kd', grad_scores, query_head, preferred_element_type=j...]
    all_to_all x4 -> x0, blocking collectives: 129 us -> none  [the longest x1 115 us: per_device(): lax.all_to_all(qkv_rows.reshape(row_count, 3, seq_count, head_cols), 'seq...]
    pallas_call x0 -> x2, Pallas kernels: none -> 125 us  [the longest x1 123 us: per_device(): pl.pallas_call(step_kernel, out_shape=(shape((256, 768), BF), shape((256,...]
    psum x1 -> x0, blocking collectives: 113 us -> none  [per_device(): lax.psum(owned[1].astype(jnp.bfloat16), 'seq').astype(jnp.float32)]
    reshape x18 -> x0, local copies, waits for them, and re-layouts: 83.6 us -> none  [the longest x8 38.4 us: owner_major(): return grad_full.reshape(owners, -1)]
    unnamed x158 -> x8, local copies, waits for them, and re-layouts: 44 us -> 0.66 us
  transfers between devices with their start and end apart: 6 -> 0, of which waited for: 2 -> 0; matrix products, arithmetic and copies ran while one was open for 6% -> 0% of each run, Pallas kernels for 0% -> 0%
where the time goes in v1:
time: 128 us
  Pallas kernels  125 us (98%)
  local copies, waits for them, and re-layouts  1.34 us (1%)
    pallas_call x1, Pallas kernels, per_device(): pl.pallas_call(step_kernel, out_shape=(shape((256, 768), BF), shape((256,...  123 us
    pallas_call x1, Pallas kernels, per_device(): pl.pallas_call(finish_kernel, out_shape=(shape((256, 768), BF), shape((25...  2.56 us

profile of v1, /device:TPU:1, one launch (start us, length us, event | category | flops | bytes accessed | tf_op | source)
XLA Modules:
  0.0 127.6 jit_solution(10977324448965122425)
XLA Ops:
  0.6 0.0 copy-start.3
  0.7 0.0 copy-start
  0.7 0.0 copy-start.1
  0.7 0.0 copy-start.2
  0.7 0.6 copy-done.3
  1.3 0.0 copy-done
  1.3 0.0 copy-done.1
  1.3 0.0 copy-done.2
  1.3 0.7 concatenate.3
  2.0 122.9 %shard_map.204 = (bf16[256,768]{1,0:T(8,128)(2,1)}, f32[256,768]{1,0:T(8,128)}, f32[2,37,8,128]{3,2,1,0:T(8,128)}) custom-call(bf16[256,768]{1,0:T(8,128)(2,1)} %bitcast.9, bf16[256,768]{1,0:T(8,128)(2,1)} %bitcast.10, s32[1,2]{1,0:T(1,128)} %refs_2_.1, s32[1,512]{1,0:T(1,128)} %refs_3_.1, bf16[256,768]{1,0:T(8,128)(2,1)} %constant.4.clone.refs_4_, ...), custom_call_target="tpu_custom_call" | custom-call | tf_op jit(solution)/shard_map/pallas_call | solution.py:1288
  124.9 2.6 %shard_map.205 = (bf16[256,768]{1,0:T(8,128)(2,1)}, f32[256,768]{1,0:T(8,128)}, f32[6,2304]{1,0:T(8,128)}, f32[6,768]{1,0:T(8,128)}, f32[6,3072]{1,0:T(8,128)}, ...) custom-call(bf16[256,768]{1,0:T(8,128)(2,1)} %get-tuple-element.23.out_in, ...), custom_call_target="tpu_custom_call" | custom-call | tf_op jit(solution)/shard_map/pallas_call | solution.py:1299
  (1 shorter events, 0.0 us)
Async XLA Ops:
  0.6 0.7 copy-start.3
  0.7 0.7 copy-start
  0.7 0.7 copy-start.1
  0.7 0.7 copy-start.2

commit v2 on v1

--- a/solution.py
+++ b/solution.py
@@ -42,7 +42,7 @@
         return self.first[st] + 3 * self.ny[st] + i
 
 
-GATHER = Split((1, 2), (5, 8), (4, 8), (0, 0), (1, 1), (0, 0))
+GATHER = Split((1, 2), (5, 9), (4, 7), (0, 0), (1, 1), (0, 0))
 REDUCE = Split((2, 1), (9, 4), (8, 4), (0, 0), (1, 1), (0, 0))
 
 
@@ -343,17 +343,23 @@
     return out
 
 
+def column(ref, step, first):
+    lane = lax.broadcasted_iota(jnp.int32, (6, 6 * step), 1)
+    row = lax.broadcasted_iota(jnp.int32, (6, 6 * step), 0)
+    values = jnp.broadcast_to(ref[...].astype(F32), (6, 6 * step))
+    return jnp.sum(jnp.where(lane == step * row + first, values, 0.0), axis=1, keepdims=True)
+
+
 def fill_slab(c, r):
     zero = jnp.zeros((2, 128), BF)
 
     def vectors():
         lane = lax.broadcasted_iota(jnp.int32, (6, 128), 1)
-        row = lax.broadcasted_iota(jnp.int32, (6, 128), 0)
-        values = jnp.broadcast_to(r.vec[...].astype(F32), (6, 128))
         total = jnp.zeros((6, 128), F32)
-        for col, at in [(0, row), (1, row + 6), (2, row + 12)] + [(4 + k, 18 + 4 * row + k) for k in range(4)]:
-            v = jnp.sum(jnp.where(lane == at, values, 0.0), axis=1, keepdims=True)
-            total = jnp.where(lane == col, v, total)
+        for col, ref in ((0, r.gain_one), (1, r.gain_two), (2, r.down_bias)):
+            total = jnp.where(lane == col, column(ref, 1, 0), total)
+        for k in range(4):
+            total = jnp.where(lane == 4 + k, column(r.up_bias, 4, k), total)
         return total.astype(BF)
 
     def tile(n):
@@ -1198,16 +1204,19 @@
 
 
 SCHEDULE = (
-    77, 0, 1, 2, 97, 78, 3, 85, 90, 79, 98, 91, 80, 86, 105, 110, 99, 81, 106, 82, 87, 92, 111, 100, 88, 93, 94, 107,
-    101, 112, 89, 83, 95, 102, 84, 113, 96, 4, 5, 114, 108, 6, 7, 8, 9, 10, 11, 12, 13, 14, 15, 16, 17, 109, 63, 103,
-    115, 18, 104, 39, 116, 19, 20, 21, 22, 23, 24, 25, 26, 27, 28, 29, 30, 31, 32, 33, 34, 35, 36, 37, 38, 40, 41,
-    42, 43, 44, 45, 123, 117, 130, 73, 46, 47, 48, 49, 50, 51, 52, 53, 54, 55, 56, 131, 57, 58, 59, 60, 61, 62, 64,
-    65, 66, 118, 67, 68, 140, 153, 146, 124, 132, 133, 69, 70, 71, 72, 74, 154, 75, 141, 134, 147, 119, 125, 155,
-    156, 76, 142, 157, 148, 126, 120, 135, 143, 149, 127, 144, 150, 158, 121, 136, 128, 122, 151, 137, 145, 159, 152,
-    129, 138, 160, 161, 139, 162,
+    77, 0, 1, 97, 2, 78, 3, 85, 90, 79, 98, 99, 110, 105, 91, 80, 86, 81, 106, 100, 111, 92, 87, 82, 107, 88, 93, 94,
+    101, 112, 83, 89, 95, 102, 113, 114, 84, 108, 96, 4, 5, 6, 7, 8, 9, 10, 11, 12, 13, 115, 14, 15, 16, 17, 109, 63,
+    103, 18, 116, 39, 104, 19, 20, 21, 22, 23, 24, 25, 26, 27, 28, 29, 30, 31, 32, 33, 34, 35, 36, 37, 38, 40, 41,
+    42, 43, 44, 45, 117, 130, 123, 73, 46, 47, 48, 49, 50, 51, 52, 53, 54, 131, 55, 56, 57, 58, 59, 60, 61, 62, 118,
+    64, 65, 66, 67, 68, 140, 153, 146, 124, 132, 133, 69, 70, 71, 72, 74, 75, 154, 134, 119, 147, 141, 125, 155, 156,
+    142, 157, 76, 148, 120, 126, 135, 143, 149, 127, 121, 144, 158, 136, 150, 122, 128, 145, 159, 151, 137, 129, 138,
+    152, 160, 161, 139, 162,
 )
 
-INPUTS = ("hidden", "d_out", "lengths", "source", "table", "qkv", "out", "up", "down", "vec")
+INPUTS = (
+    "hidden", "d_out", "lengths", "source", "table", "qkv", "out", "up", "down",
+    "gain_one", "gain_two", "down_bias", "up_bias",
+)
 OUTPUTS = ("output", "grad_hidden", "done")
 BUFFERS = {
     "W": ((NT, 4, 4, 48, 128), BF),
@@ -1238,10 +1247,11 @@
 
 
 def finish_kernel(
-    out_in, hidden_in, done, qkv, up, vec, out, hidden, gqkv, gout, gup, gdown, g1, g2, gub, gdb
+    out_in, hidden_in, done, qkv, up, gain_one, gain_two, out, hidden, gqkv, gout, gup, gdown, g1, g2, gub, gdb, sems
 ):
-    out[...] = out_in[...]
-    hidden[...] = hidden_in[...]
+    copies = [pltpu.make_async_copy(out_in, out, sems.at[0]), pltpu.make_async_copy(hidden_in, hidden, sems.at[1])]
+    for copy in copies:
+        copy.start()
     for core in range(2):
         for i, t in enumerate(GQKV):
             n = (i // 3) * 768 + core * 384 + (i % 3) * 128
@@ -1254,7 +1264,6 @@
     row = lax.broadcasted_iota(jnp.int32, (6, 128), 0)
     one = done[0, GVEC, 0:6]
     both = one + done[1, GVEC, 0:6]
-    values = jnp.broadcast_to(vec[...].astype(F32), (6, 128))
 
     def as_row(places):
         total = jnp.zeros((6, 128), F32)
@@ -1262,17 +1271,19 @@
             total = jnp.where(lane == at, v, total)
         return jnp.sum(total, axis=0)
 
-    def gain_grad(weight, grad, first):
-        gain = jnp.sum(jnp.where(lane == row + first, values, 0.0), axis=1, keepdims=True)
-        return jnp.sum(weight[...].astype(F32) * grad[...], axis=1, keepdims=True) / gain
-
-    g1[...] = as_row([(gain_grad(qkv, gqkv, 0), row)])[0:6]
-    g2[...] = as_row([(gain_grad(up, gup, 6), row)])[0:6]
+    def gain_grad(weight, grad, gain):
+        return jnp.sum(weight[...].astype(F32) * grad[...], axis=1, keepdims=True) / column(gain, 1, 0)
+
+    g1[...] = as_row([(gain_grad(qkv, gqkv, gain_one), row)])[0:6]
+    g2[...] = as_row([(gain_grad(up, gup, gain_two), row)])[0:6]
     gdb[...] = as_row([(one[:, 2:3], row)])[0:6]
     gub[...] = as_row([(both[:, 4 + k : 5 + k], 4 * row + k) for k in range(4)])[0:24]
+    for copy in copies:
+        copy.wait()
 
 
 VM = pl.BlockSpec(memory_space=pltpu.VMEM)
+ANY = pl.BlockSpec(memory_space=pl.ANY)
 LIMIT = 62 * 2**20
 
 
@@ -1284,17 +1295,17 @@
     hidden, d_out, lengths, slot_source, first_gain, qkv_weight, out_weight, second_gain, up_weight, up_bias,
     down_weight, down_bias,
 ):
-    vec = jnp.concatenate([first_gain, second_gain, down_bias, up_bias, jnp.zeros((86,), BF)])[None]
     parts = pl.pallas_call(
         step_kernel,
         out_shape=(shape((256, 768), BF), shape((256, 768)), shape((2, NT, 8, 128))),
-        in_specs=[VM, VM, pl.BlockSpec(memory_space=pltpu.SMEM)] + [VM] * 7,
+        in_specs=[VM, VM, pl.BlockSpec(memory_space=pltpu.SMEM)] + [VM] * 10,
         out_specs=(VM,) * 3,
         scratch_shapes=[pltpu.VMEM(*v) for v in BUFFERS.values()] + [pltpu.SemaphoreType.DMA((SEMS,))] * 2,
         compiler_params=pltpu.CompilerParams(collective_id=0, has_side_effects=True, vmem_limit_bytes=LIMIT),
     )(
         hidden[0], d_out[0], lengths, slot_source, rotary_table(),
-        qkv_weight, out_weight.T, up_weight, down_weight.T, vec,
+        qkv_weight, out_weight.T, up_weight, down_weight.T,
+        first_gain[None], second_gain[None], down_bias[None], up_bias[None],
     )
     output, grad_hidden, gqkv, gout, gup, gdown, g1, g2, gub, gdb = pl.pallas_call(
         finish_kernel,
@@ -1310,9 +1321,10 @@
             shape((24,)),
             shape((6,)),
         ),
-        in_specs=[VM] * 6,
-        out_specs=(VM,) * 10,
-    )(*parts, qkv_weight, up_weight, vec)
+        in_specs=[ANY] * 2 + [VM] * 5,
+        out_specs=(ANY,) * 2 + (VM,) * 8,
+        scratch_shapes=[pltpu.SemaphoreType.DMA((2,))],
+    )(*parts, qkv_weight, up_weight, first_gain[None], second_gain[None])
     return (output[None], grad_hidden[None], g1, gqkv, gout.T, g2, gup, gub, gdown.T, gdb)
 
 

time: 128 us -> 165 us (1.29)
  Pallas kernels: 125 us -> 164 us
    pallas_call x1, Pallas kernels: 2.56 us -> 38.6 us  [per_device(): pl.pallas_call(finish_kernel, out_shape=(shape((256, 768), BF), shape((25...]
    pallas_call x1, Pallas kernels: 123 us -> 126 us  [per_device(): pl.pallas_call(step_kernel, out_shape=(shape((256, 768), BF), shape((256,...]
where the time goes in v2:
time: 165 us
  Pallas kernels  164 us (99%)
    pallas_call x1, Pallas kernels, per_device(): pl.pallas_call(step_kernel, out_shape=(shape((256, 768), BF), shape((256,...  126 us
    pallas_call x1, Pallas kernels, per_device(): pl.pallas_call(finish_kernel, out_shape=(shape((256, 768), BF), shape((25...  38.6 us

profile of v2, /device:TPU:1, one launch (start us, length us, event | category | flops | bytes accessed | tf_op | source)
XLA Modules:
  0.0 165.0 jit_solution(8955292913279514142)
XLA Ops:
  0.6 125.5 %shard_map.204 = (bf16[256,768]{1,0:T(8,128)(2,1)}, f32[256,768]{1,0:T(8,128)}, f32[2,37,8,128]{3,2,1,0:T(8,128)}) custom-call(bf16[256,768]{1,0:T(8,128)(2,1)} %bitcast.12, bf16[256,768]{1,0:T(8,128)(2,1)} %bitcast.13, s32[1,2]{1,0:T(1,128)} %refs_2_.1, s32[1,512]{1,0:T(1,128)} %refs_3_.1, bf16[256,768]{1,0:T(8,128)(2,1)} %constant.2.clone.refs_4_, ...), custom_call_target="tpu_custom_call" | custom-call | tf_op jit(solution)/shard_map/pallas_call | solution.py:1298
  126.2 38.6 %shard_map.205 = (bf16[256,768]{1,0:T(8,128)(2,1)}, f32[256,768]{1,0:T(8,128)}, f32[6,2304]{1,0:T(8,128)}, f32[6,768]{1,0:T(8,128)}, f32[6,3072]{1,0:T(8,128)}, ...) custom-call(bf16[256,768]{1,0:T(8,128)(2,1)} %get-tuple-element.23.out_in, ...), custom_call_target="tpu_custom_call" | custom-call | tf_op jit(solution)/shard_map/pallas_call | solution.py:1310

commit v3 on v2

--- a/solution.py
+++ b/solution.py
@@ -42,7 +42,7 @@
         return self.first[st] + 3 * self.ny[st] + i
 
 
-GATHER = Split((1, 2), (5, 9), (4, 7), (0, 0), (1, 1), (0, 0))
+GATHER = Split((1, 2), (5, 8), (4, 8), (0, 0), (1, 1), (0, 0))
 REDUCE = Split((2, 1), (9, 4), (8, 4), (0, 0), (1, 1), (0, 0))
 
 
@@ -1204,13 +1204,13 @@
 
 
 SCHEDULE = (
-    77, 0, 1, 97, 2, 78, 3, 85, 90, 79, 98, 99, 110, 105, 91, 80, 86, 81, 106, 100, 111, 92, 87, 82, 107, 88, 93, 94,
-    101, 112, 83, 89, 95, 102, 113, 114, 84, 108, 96, 4, 5, 6, 7, 8, 9, 10, 11, 12, 13, 115, 14, 15, 16, 17, 109, 63,
-    103, 18, 116, 39, 104, 19, 20, 21, 22, 23, 24, 25, 26, 27, 28, 29, 30, 31, 32, 33, 34, 35, 36, 37, 38, 40, 41,
-    42, 43, 44, 45, 117, 130, 123, 73, 46, 47, 48, 49, 50, 51, 52, 53, 54, 131, 55, 56, 57, 58, 59, 60, 61, 62, 118,
-    64, 65, 66, 67, 68, 140, 153, 146, 124, 132, 133, 69, 70, 71, 72, 74, 75, 154, 134, 119, 147, 141, 125, 155, 156,
-    142, 157, 76, 148, 120, 126, 135, 143, 149, 127, 121, 144, 158, 136, 150, 122, 128, 145, 159, 151, 137, 129, 138,
-    152, 160, 161, 139, 162,
+    77, 0, 1, 2, 97, 78, 3, 85, 90, 79, 98, 91, 80, 86, 105, 110, 99, 81, 106, 82, 87, 92, 111, 100, 88, 93, 94, 107,
+    101, 112, 89, 83, 95, 102, 84, 113, 96, 4, 5, 114, 108, 6, 7, 8, 9, 10, 11, 12, 13, 14, 15, 16, 17, 109, 63, 103,
+    115, 18, 104, 39, 116, 19, 20, 21, 22, 23, 24, 25, 26, 27, 28, 29, 30, 31, 32, 33, 34, 35, 36, 37, 38, 40, 41,
+    42, 43, 44, 45, 123, 117, 130, 73, 46, 47, 48, 49, 50, 51, 52, 53, 54, 55, 56, 131, 57, 58, 59, 60, 61, 62, 64,
+    65, 66, 118, 67, 68, 140, 153, 146, 124, 132, 133, 69, 70, 71, 72, 74, 154, 75, 141, 134, 147, 119, 125, 155,
+    156, 76, 142, 157, 148, 126, 120, 135, 143, 149, 127, 144, 150, 158, 121, 136, 128, 122, 151, 137, 145, 159, 152,
+    129, 138, 160, 161, 139, 162,
 )
 
 INPUTS = (
@@ -1247,11 +1247,10 @@
 
 
 def finish_kernel(
-    out_in, hidden_in, done, qkv, up, gain_one, gain_two, out, hidden, gqkv, gout, gup, gdown, g1, g2, gub, gdb, sems
+    out_in, hidden_in, done, qkv, up, gain_one, gain_two, out, hidden, gqkv, gout, gup, gdown, g1, g2, gub, gdb
 ):
-    copies = [pltpu.make_async_copy(out_in, out, sems.at[0]), pltpu.make_async_copy(hidden_in, hidden, sems.at[1])]
-    for copy in copies:
-        copy.start()
+    out[...] = out_in[...]
+    hidden[...] = hidden_in[...]
     for core in range(2):
         for i, t in enumerate(GQKV):
             n = (i // 3) * 768 + core * 384 + (i % 3) * 128
@@ -1278,12 +1277,9 @@
     g2[...] = as_row([(gain_grad(up, gup, gain_two), row)])[0:6]
     gdb[...] = as_row([(one[:, 2:3], row)])[0:6]
     gub[...] = as_row([(both[:, 4 + k : 5 + k], 4 * row + k) for k in range(4)])[0:24]
-    for copy in copies:
-        copy.wait()
 
 
 VM = pl.BlockSpec(memory_space=pltpu.VMEM)
-ANY = pl.BlockSpec(memory_space=pl.ANY)
 LIMIT = 62 * 2**20
 
 
@@ -1321,9 +1317,8 @@
             shape((24,)),
             shape((6,)),
         ),
-        in_specs=[ANY] * 2 + [VM] * 5,
-        out_specs=(ANY,) * 2 + (VM,) * 8,
-        scratch_shapes=[pltpu.SemaphoreType.DMA((2,))],
+        in_specs=[VM] * 7,
+        out_specs=(VM,) * 10,
     )(*parts, qkv_weight, up_weight, first_gain[None], second_gain[None])
     return (output[None], grad_hidden[None], g1, gqkv, gout.T, g2, gup, gub, gdown.T, gdb)
 

time: 165 us -> 127 us (0.77)
  Pallas kernels: 164 us -> 126 us
    pallas_call x1, Pallas kernels: 38.6 us -> 2.58 us  [per_device(): pl.pallas_call(finish_kernel, out_shape=(shape((256, 768), BF), shape((25...]
    pallas_call x1, Pallas kernels: 126 us -> 123 us  [per_device(): pl.pallas_call(step_kernel, out_shape=(shape((256, 768), BF), shape((256,...]
where the time goes in v3:
time: 127 us; the launch traced here: 126 us
  Pallas kernels  126 us (99%)
    pallas_call x1, Pallas kernels, per_device(): pl.pallas_call(step_kernel, out_shape=(shape((256, 768), BF), shape((256,...  123 us
    pallas_call x1, Pallas kernels, per_device(): pl.pallas_call(finish_kernel, out_shape=(shape((256, 768), BF), shape((25...  2.58 us

profile of v3, /device:TPU:1, one launch (start us, length us, event | category | flops | bytes accessed | tf_op | source)
XLA Modules:
  0.0 126.5 jit_solution(13092988063590533508)
XLA Ops:
  0.6 123.1 %shard_map.204 = (bf16[256,768]{1,0:T(8,128)(2,1)}, f32[256,768]{1,0:T(8,128)}, f32[2,37,8,128]{3,2,1,0:T(8,128)}) custom-call(bf16[256,768]{1,0:T(8,128)(2,1)} %bitcast.12, bf16[256,768]{1,0:T(8,128)(2,1)} %bitcast.13, s32[1,2]{1,0:T(1,128)} %refs_2_.1, s32[1,512]{1,0:T(1,128)} %refs_3_.1, bf16[256,768]{1,0:T(8,128)(2,1)} %constant.2.clone.refs_4_, ...), custom_call_target="tpu_custom_call" | custom-call | tf_op jit(solution)/shard_map/pallas_call | solution.py:1294
  123.7 2.6 %shard_map.205 = (bf16[256,768]{1,0:T(8,128)(2,1)}, f32[256,768]{1,0:T(8,128)}, f32[6,2304]{1,0:T(8,128)}, f32[6,768]{1,0:T(8,128)}, f32[6,3072]{1,0:T(8,128)}, ...) custom-call(bf16[256,768]{1,0:T(8,128)(2,1)} %get-tuple-element.23.out_in, ...), custom_call_target="tpu_custom_call" | custom-call | tf_op jit(solution)/shard_map/pallas_call | solution.py:1306
